TPU v7x, 512 devices: a whole 4x4x16 slice. The times are simulated.
512 devices in a mesh: inter: 16 (over z), intra: 32 (over y, x, core).
Axes of the slice: x: 4, y: 4, z: 16, core: 2. Of those that a mesh axis runs over, the one named last changes fastest.
Arguments:
- tokens: bfloat16 [65536, 768], P(('inter', 'intra')), may hold values from -6 to 6
- expert_ids: int32 [65536], P(('inter', 'intra')), may hold values from 0 to 63
- slot_ids: int32 [65536], P(('inter', 'intra')), may hold values from 0 to 1, as said below
- keep_mask: int32 [65536], P(('inter', 'intra')), may hold values from 0 to 1, as said below
- gate_prob: float32 [65536], P(('inter', 'intra')), may hold values from 0.25 to 1
- out_grad: bfloat16 [65536, 768], P(('inter', 'intra')), may hold values from -1.5 to 1.5
- in_weight: bfloat16 [16, 32, 768, 384], P('inter', 'intra'), may hold values from -0.21875 to 0.21875
- out_weight: bfloat16 [16, 32, 384, 768], P('inter', 'intra'), may hold values from -0.109375 to 0.109375
Outputs:
- expert_out: bfloat16 [65536, 768], P(('inter', 'intra'))
- gate_grad: float32 [65536], P(('inter', 'intra'))
- token_grad: bfloat16 [65536, 768], P(('inter', 'intra'))
- in_weight_grad: bfloat16 [16, 32, 768, 384], P('inter', 'intra')
- out_weight_grad: bfloat16 [16, 32, 384, 768], P('inter', 'intra')
Inputs may be any that keep to these rules, and one draw needn't show every extreme that they name: `slot_ids`: within the rows of one device, a token's slot is the number of earlier tokens of that device with the same expert, capped at 1; kept tokens of one device have distinct expert and slot pairs. One expert has more than 2 tokens in the rows of every device. `keep_mask`: 1 exactly where fewer than 2 earlier tokens of the same device chose the same expert.
All inputs are finite; a program needn't handle non-finite values.
Results may differ from a plain program's by a relative error of at most 0.0064.
Values may be sent and summed in bfloat16 or wider, within the bound.
No kernel may reach another device: no remote copies, remote signals or barrier semaphores. Data moves between devices by JAX's collectives and lax.ppermute only.
A program may use at most 64 MiB of HBM per device.

v0:
```python
import math

import jax
import jax.numpy as jnp
from jax import lax
from jax.sharding import PartitionSpec as P

EGRP = 2


gelu_root = math.sqrt(2.0 / math.pi)
gelu_cubic = 0.044715


def gelu(pre_value):
    argument = gelu_root * (pre_value + gelu_cubic * pre_value * pre_value * pre_value)
    return 0.5 * pre_value * (1.0 + jnp.tanh(argument))


def gelu_slope(pre_value):
    argument = gelu_root * (pre_value + gelu_cubic * pre_value * pre_value * pre_value)
    slope_tanh = jnp.tanh(argument)
    return 0.5 * (1.0 + slope_tanh) + 0.5 * pre_value * (
        1.0 - slope_tanh * slope_tanh
    ) * gelu_root * (1.0 + 3.0 * gelu_cubic * pre_value * pre_value)


def spread_slots(buffer, blocks_ff):
    moved = lax.all_to_all(buffer, "intra", split_axis=1, concat_axis=1, tiled=True)
    copies = jnp.broadcast_to(moved[:, None], (EGRP, blocks_ff) + moved.shape[1:])
    copies = copies.reshape((EGRP * blocks_ff,) + moved.shape[1:])
    return lax.all_to_all(copies, "inter", split_axis=0, concat_axis=0, tiled=True)


def send_home(partial_value, blocks_ff):
    arrived = lax.all_to_all(partial_value, "inter", split_axis=0, concat_axis=0, tiled=True)
    shaped = arrived.reshape((EGRP, blocks_ff) + arrived.shape[1:])
    summed = jnp.sum(shaped, axis=1, dtype=jnp.float32).astype(jnp.bfloat16)
    return lax.all_to_all(summed, "intra", split_axis=1, concat_axis=1, tiled=True)


def on_device(tokens, expert_ids, slot_ids, keep_mask, gate_prob, out_grad, in_weight, out_weight):
    tok_rows, model_width = tokens.shape
    intra_size = lax.axis_size("intra")
    inter_size = lax.axis_size("inter")
    blocks_ff = inter_size // EGRP
    experts = EGRP * intra_size
    capacity = max(2, tok_rows * 5 // 4 // experts)
    weight_in = in_weight[0, 0]
    weight_out = out_weight[0, 0]
    columns = expert_ids * capacity + slot_ids
    one_hot = (
        (columns[:, None] == jnp.arange(experts * capacity)[None, :]) & (keep_mask[:, None] == 1)
    ).astype(jnp.bfloat16)

    def to_slots(values):
        placed = jnp.einsum("tc,td->cd", one_hot, values, preferred_element_type=jnp.float32)
        return placed.astype(jnp.bfloat16).reshape(EGRP, intra_size, capacity, model_width)

    def from_slots(buffer):
        flat = buffer.reshape(experts * capacity, model_width)
        return jnp.dot(one_hot, flat, preferred_element_type=jnp.float32)

    dispatched = to_slots(tokens)
    slot_rows = spread_slots(dispatched, blocks_ff)
    pre_act = jnp.einsum("abcd,df->abcf", slot_rows, weight_in, preferred_element_type=jnp.float32)
    hidden = gelu(pre_act).astype(jnp.bfloat16)
    partial_out = jnp.einsum(
        "abcf,fd->abcd", hidden, weight_out, preferred_element_type=jnp.float32
    ).astype(jnp.bfloat16)
    returned = send_home(partial_out, blocks_ff)
    ffn_tok = from_slots(returned)
    expert_out = (gate_prob[:, None] * ffn_tok).astype(jnp.bfloat16)
    gate_grad = jnp.sum(out_grad.astype(jnp.float32) * ffn_tok, axis=1)
    scaled_grad = (gate_prob[:, None] * out_grad.astype(jnp.float32)).astype(jnp.bfloat16)
    grad_rows = spread_slots(to_slots(scaled_grad), blocks_ff)
    input_rows = spread_slots(dispatched, blocks_ff)
    hidden_grad = jnp.einsum(
        "abcd,fd->abcf", grad_rows, weight_out, preferred_element_type=jnp.float32
    )
    pre_grad = (hidden_grad * gelu_slope(pre_act)).astype(jnp.bfloat16)
    out_weight_grad = jnp.einsum(
        "abcf,abcd->fd", hidden, grad_rows, preferred_element_type=jnp.float32
    ).astype(jnp.bfloat16)
    in_weight_grad = jnp.einsum(
        "abcd,abcf->df", input_rows, pre_grad, preferred_element_type=jnp.float32
    ).astype(jnp.bfloat16)
    partial_in = jnp.einsum(
        "abcf,df->abcd", pre_grad, weight_in, preferred_element_type=jnp.float32
    ).astype(jnp.bfloat16)
    returned_grad = send_home(partial_in, blocks_ff)
    token_grad = from_slots(returned_grad).astype(jnp.bfloat16)
    return (
        expert_out,
        gate_grad,
        token_grad,
        in_weight_grad[None, None],
        out_weight_grad[None, None],
    )


def solution(mesh):
    return jax.shard_map(
        on_device,
        mesh=mesh,
        in_specs=(
            P(("inter", "intra"), None),
            P(("inter", "intra")),
            P(("inter", "intra")),
            P(("inter", "intra")),
            P(("inter", "intra")),
            P(("inter", "intra"), None),
            P("inter", "intra", None, None),
            P("inter", "intra", None, None),
        ),
        out_specs=(
            P(("inter", "intra"), None),
            P(("inter", "intra")),
            P(("inter", "intra"), None),
            P("inter", "intra", None, None),
            P("inter", "intra", None, None),
        ),
        check_vma=False,
    )
```

profile of v0, /device:TPU:1, one launch (start us, length us, event | category | flops | bytes accessed | tf_op | source)
XLA Modules:
  0.0 394.0 jit_solution(8185034113416646037)
XLA Ops:
  0.6 0.0 copy-start
  0.6 0.0 copy-start.2
  0.7 0.0 copy-start.4
  0.7 0.7 broadcast_compare_fusion
  1.4 0.7 multiply_add_fusion.1
  2.1 1.3 convolution_convert_fusion.4
  3.3 0.1 reshape.41
  3.4 0.8 copy.21
  4.2 10.4 %all-to-all-start = ((bf16[2,32,2,768]{3,2,0,1:T(2,128)(2,1)}), bf16[2,32,2,768]{3,2,0,1:T(2,128)(2,1)S(1)}, u32[]{:S(2)}, u32[]{:S(2)}) async-start(bf16[2,32,2,768]{3,2,0,1:T(2,128)(2,1)} %copy.21), calls=%async_computation | async-start | bytes 393216 | tf_op jit(solution)/shard_map/all_to_all | solution.py:29
  14.7 0.3 convolution_convert_fusion.3
  15.0 0.1 reshape.45
  15.1 0.8 copy.25
  15.9 7.1 %all-to-all-done = bf16[2,32,2,768]{3,2,0,1:T(2,128)(2,1)S(1)} async-done(((bf16[2,32,2,768]{3,2,0,1:T(2,128)(2,1)}), bf16[2,32,2,768]{3,2,0,1:T(2,128)(2,1)S(1)}, u32[]{:S(2)}, u32[]{:S(2)}) %all-to-all-start) | async-done | bytes 196640 | tf_op jit(solution)/shard_map/all_to_all | solution.py:29
  23.0 3.8 all-to-all-start.4
  26.9 8.2 %all-to-all-done.4 = bf16[2,32,2,768]{3,2,0,1:T(2,128)(2,1)S(1)} async-done(((bf16[2,32,2,768]{3,2,0,1:T(2,128)(2,1)}), bf16[2,32,2,768]{3,2,0,1:T(2,128)(2,1)S(1)}, u32[]{:S(2)}, u32[]{:S(2)}) %all-to-all-start.4) | async-done | bytes 196640 | tf_op jit(solution)/shard_map/all_to_all | solution.py:29
  35.1 1.4 broadcast_in_dim.8
  36.4 13.0 %all-to-all-start.1 = ((bf16[16,32,2,768]{3,1,2,0:T(8,128)(2,1)}), bf16[16,32,2,768]{3,1,2,0:T(8,128)(2,1)S(1)}, u32[]{:S(2)}, u32[]{:S(2)}) async-start(bf16[16,32,2,768]{3,1,2,0:T(8,128)(2,1)} %bitcast.53), calls=%async_computation.1 | async-start | bytes 3145728 | tf_op jit(solution)/shard_map/all_to_all | solution.py:32
  49.5 69.3 %all-to-all-done.1 = bf16[16,32,2,768]{3,1,2,0:T(8,128)(2,1)S(1)} async-done(((bf16[16,32,2,768]{3,1,2,0:T(8,128)(2,1)}), bf16[16,32,2,768]{3,1,2,0:T(8,128)(2,1)S(1)}, u32[]{:S(2)}, u32[]{:S(2)}) %all-to-all-start.1) | async-done | bytes 1572896 | tf_op jit(solution)/shard_map/all_to_all | solution.py:32
  118.7 1.3 broadcast_in_dim.9
  120.1 11.4 %all-to-all-start.5 = ((bf16[16,32,2,768]{3,1,2,0:T(8,128)(2,1)}), bf16[16,32,2,768]{3,1,2,0:T(8,128)(2,1)}, u32[]{:S(2)}, u32[]{:S(2)}) async-start(bf16[16,32,2,768]{3,1,2,0:T(8,128)(2,1)} %bitcast.54), calls=%async_computation.5 | async-start | bytes 3145728 | tf_op jit(solution)/shard_map/all_to_all | solution.py:32
  131.5 1.0 fusion.12
  132.5 0.0 copy-start.1
  132.5 1.1 copy-done.1
  133.7 2.4 convolution_convert_fusion.1
  136.1 64.5 %all-to-all-done.5 = bf16[16,32,2,768]{3,1,2,0:T(8,128)(2,1)} async-done(((bf16[16,32,2,768]{3,1,2,0:T(8,128)(2,1)}), bf16[16,32,2,768]{3,1,2,0:T(8,128)(2,1)}, u32[]{:S(2)}, u32[]{:S(2)}) %all-to-all-start.5) | async-done | bytes 1572896 | tf_op jit(solution)/shard_map/all_to_all | solution.py:32
  200.5 11.6 %all-to-all-start.2 = ((bf16[16,32,2,768]{3,1,2,0:T(8,128)(2,1)}), bf16[16,32,2,768]{3,1,2,0:T(8,128)(2,1)}, u32[]{:S(2)}, u32[]{:S(2)}) async-start(bf16[16,32,2,768]{3,1,2,0:T(8,128)(2,1)} %convolution_convert_fusion.1), calls=%async_computation.2 | async-start | bytes 3145728 | tf_op jit(solution)/shard_map/all_to_all | solution.py:36
  212.1 3.5 fusion.6
  215.7 1.0 copy-done.5
  216.6 2.2 convolution_convert_fusion
  218.8 62.4 %all-to-all-done.2 = bf16[16,32,2,768]{3,1,2,0:T(8,128)(2,1)} async-done(((bf16[16,32,2,768]{3,1,2,0:T(8,128)(2,1)}), bf16[16,32,2,768]{3,1,2,0:T(8,128)(2,1)}, u32[]{:S(2)}, u32[]{:S(2)}) %all-to-all-start.2) | async-done | bytes 1572896 | tf_op jit(solution)/shard_map/all_to_all | solution.py:36
  281.2 11.6 %all-to-all-start.6 = ((bf16[16,32,2,768]{3,1,2,0:T(8,128)(2,1)}), bf16[16,32,2,768]{3,1,2,0:T(8,128)(2,1)}, u32[]{:S(2)}, u32[]{:S(2)}) async-start(bf16[16,32,2,768]{3,1,2,0:T(8,128)(2,1)} %convolution_convert_fusion), calls=%async_computation.6 | async-start | bytes 3145728 | tf_op jit(solution)/shard_map/all_to_all | solution.py:36
  292.8 3.7 fusion.9
  296.4 1.6 bitcast_reduce_fusion.1
  298.1 0.9 copy.23
  298.9 62.9 %all-to-all-done.6 = bf16[16,32,2,768]{3,1,2,0:T(8,128)(2,1)} async-done(((bf16[16,32,2,768]{3,1,2,0:T(8,128)(2,1)}), bf16[16,32,2,768]{3,1,2,0:T(8,128)(2,1)}, u32[]{:S(2)}, u32[]{:S(2)}) %all-to-all-start.6) | async-done | bytes 1572896 | tf_op jit(solution)/shard_map/all_to_all | solution.py:36
  361.8 9.8 %all-to-all-start.3 = ((bf16[2,32,2,768]{3,2,0,1:T(2,128)(2,1)}), bf16[2,32,2,768]{3,2,0,1:T(2,128)(2,1)S(1)}, u32[]{:S(2)}, u32[]{:S(2)}) async-start(bf16[2,32,2,768]{3,2,0,1:T(2,128)(2,1)} %copy.23), calls=%async_computation.3 | async-start | bytes 393216 | tf_op jit(solution)/shard_map/all_to_all | solution.py:39
  371.6 3.0 fusion.10
  374.6 1.6 bitcast_reduce_fusion
  376.2 0.9 copy.27
  377.1 2.9 all-to-all-done.3
  380.0 4.6 %all-to-all-start.7 = ((bf16[2,32,2,768]{3,2,0,1:T(2,128)(2,1)}), bf16[2,32,2,768]{3,2,0,1:T(2,128)(2,1)S(1)}, u32[]{:S(2)}, u32[]{:S(2)}) async-start(bf16[2,32,2,768]{3,2,0,1:T(2,128)(2,1)} %copy.27), calls=%async_computation.7 | async-start | bytes 393216 | tf_op jit(solution)/shard_map/all_to_all | solution.py:39
  384.6 0.1 copy.24
  384.7 0.1 reshape.44
  384.8 1.5 fusion.16
  386.3 6.6 %all-to-all-done.7 = bf16[2,32,2,768]{3,2,0,1:T(2,128)(2,1)S(1)} async-done(((bf16[2,32,2,768]{3,2,0,1:T(2,128)(2,1)}), bf16[2,32,2,768]{3,2,0,1:T(2,128)(2,1)S(1)}, u32[]{:S(2)}, u32[]{:S(2)}) %all-to-all-start.7) | async-done | bytes 196640 | tf_op jit(solution)/shard_map/all_to_all | solution.py:39
  392.9 0.1 copy.28
  393.0 0.1 reshape.48
  393.1 0.9 convolution_convert_fusion.2
  (8 shorter events, 0.1 us)
Async XLA Ops:
  0.6 133.0 %copy-start = (bf16[1,1,384,768]{3,2,1,0:T(8,128)(2,1)S(1)}, bf16[1,1,384,768]{3,2,1,0:T(8,128)(2,1)}, u32[]{:S(2)}) copy-start(bf16[1,1,384,768]{3,2,1,0:T(8,128)(2,1)} %param.15) | copy-start | bytes 1769476
  0.6 14.0 %copy-start.2 = (bf16[128,768]{1,0:T(8,128)(2,1)S(1)}, bf16[128,768]{1,0:T(8,128)(2,1)}, u32[]{:S(2)}) copy-start(bf16[128,768]{1,0:T(8,128)(2,1)} %param.13) | copy-start | bytes 589828
  0.7 14.0 %copy-start.4 = (f32[128]{0:T(128)S(1)}, f32[128]{0:T(128)}, u32[]{:S(2)}) copy-start(f32[128]{0:T(128)} %param.12) | copy-start | bytes 1540
  4.2 18.8 %all-to-all-start = ((bf16[2,32,2,768]{3,2,0,1:T(2,128)(2,1)}), bf16[2,32,2,768]{3,2,0,1:T(2,128)(2,1)S(1)}, u32[]{:S(2)}, u32[]{:S(2)}) async-start(bf16[2,32,2,768]{3,2,0,1:T(2,128)(2,1)} %copy.21), calls=%async_computation | async-start | bytes 393216 | tf_op jit(solution)/shard_map/all_to_all | solution.py:29
  23.0 12.1 %all-to-all-start.4 = ((bf16[2,32,2,768]{3,2,0,1:T(2,128)(2,1)}), bf16[2,32,2,768]{3,2,0,1:T(2,128)(2,1)S(1)}, u32[]{:S(2)}, u32[]{:S(2)}) async-start(bf16[2,32,2,768]{3,2,0,1:T(2,128)(2,1)} %copy.25), calls=%async_computation.4 | async-start | bytes 393216 | tf_op jit(solution)/shard_map/all_to_all | solution.py:29
  36.4 82.3 %all-to-all-start.1 = ((bf16[16,32,2,768]{3,1,2,0:T(8,128)(2,1)}), bf16[16,32,2,768]{3,1,2,0:T(8,128)(2,1)S(1)}, u32[]{:S(2)}, u32[]{:S(2)}) async-start(bf16[16,32,2,768]{3,1,2,0:T(8,128)(2,1)} %bitcast.53), calls=%async_computation.1 | async-start | bytes 3145728 | tf_op jit(solution)/shard_map/all_to_all | solution.py:32
  120.1 11.5 %copy-start.3 = (bf16[1,1,768,384]{3,2,1,0:T(8,128)(2,1)S(1)}, bf16[1,1,768,384]{3,2,1,0:T(8,128)(2,1)}, u32[]{:S(2)}) copy-start(bf16[1,1,768,384]{3,2,1,0:T(8,128)(2,1)} %param.14) | copy-start | bytes 1769476
  120.1 80.5 %all-to-all-start.5 = ((bf16[16,32,2,768]{3,1,2,0:T(8,128)(2,1)}), bf16[16,32,2,768]{3,1,2,0:T(8,128)(2,1)}, u32[]{:S(2)}, u32[]{:S(2)}) async-start(bf16[16,32,2,768]{3,1,2,0:T(8,128)(2,1)} %bitcast.54), calls=%async_computation.5 | async-start | bytes 3145728 | tf_op jit(solution)/shard_map/all_to_all | solution.py:32
  132.5 1.1 copy-start.1
  200.5 80.6 %all-to-all-start.2 = ((bf16[16,32,2,768]{3,1,2,0:T(8,128)(2,1)}), bf16[16,32,2,768]{3,1,2,0:T(8,128)(2,1)}, u32[]{:S(2)}, u32[]{:S(2)}) async-start(bf16[16,32,2,768]{3,1,2,0:T(8,128)(2,1)} %convolution_convert_fusion.1), calls=%async_computation.2 | async-start | bytes 3145728 | tf_op jit(solution)/shard_map/all_to_all | solution.py:36
  215.7 1.0 copy-start.5
  281.2 80.6 %all-to-all-start.6 = ((bf16[16,32,2,768]{3,1,2,0:T(8,128)(2,1)}), bf16[16,32,2,768]{3,1,2,0:T(8,128)(2,1)}, u32[]{:S(2)}, u32[]{:S(2)}) async-start(bf16[16,32,2,768]{3,1,2,0:T(8,128)(2,1)} %convolution_convert_fusion), calls=%async_computation.6 | async-start | bytes 3145728 | tf_op jit(solution)/shard_map/all_to_all | solution.py:36
  361.8 18.2 %all-to-all-start.3 = ((bf16[2,32,2,768]{3,2,0,1:T(2,128)(2,1)}), bf16[2,32,2,768]{3,2,0,1:T(2,128)(2,1)S(1)}, u32[]{:S(2)}, u32[]{:S(2)}) async-start(bf16[2,32,2,768]{3,2,0,1:T(2,128)(2,1)} %copy.23), calls=%async_computation.3 | async-start | bytes 393216 | tf_op jit(solution)/shard_map/all_to_all | solution.py:39
  380.0 12.9 %all-to-all-start.7 = ((bf16[2,32,2,768]{3,2,0,1:T(2,128)(2,1)}), bf16[2,32,2,768]{3,2,0,1:T(2,128)(2,1)S(1)}, u32[]{:S(2)}, u32[]{:S(2)}) async-start(bf16[2,32,2,768]{3,2,0,1:T(2,128)(2,1)} %copy.27), calls=%async_computation.7 | async-start | bytes 393216 | tf_op jit(solution)/shard_map/all_to_all | solution.py:39
where the time goes:
time: 395 us; the launch traced here: 394 us
  waiting for transfers between devices  284 us (72%)
  starting transfers between devices  76.3 us (19%)
  matrix products  19.6 us (5%)
  local copies, waits for them, and re-layouts  8.82 us (2%)
  other arithmetic  4.65 us (1%)
    all_to_all x2, waiting for transfers between devices, spread_slots(): lax.all_to_all(copies, 'inter', split_axis=0, concat_axis=0, tiled=True)  134 us
    all_to_all x2, waiting for transfers between devices, send_home(): lax.all_to_all(partial_value, 'inter', split_axis=0, concat_axis=0, tiled...  125 us
    all_to_all x2, starting transfers between devices, spread_slots(): lax.all_to_all(copies, 'inter', split_axis=0, concat_axis=0, tiled=True)  24.4 us
    all_to_all x2, starting transfers between devices, send_home(): lax.all_to_all(partial_value, 'inter', split_axis=0, concat_axis=0, tiled...  23.2 us
    all_to_all x2, waiting for transfers between devices, spread_slots(): lax.all_to_all(buffer, 'intra', split_axis=1, concat_axis=1, tiled=True)  15.4 us
    all_to_all x2, starting transfers between devices, send_home(): lax.all_to_all(summed, 'intra', split_axis=1, concat_axis=1, tiled=True)  14.4 us
    all_to_all x2, starting transfers between devices, spread_slots(): lax.all_to_all(buffer, 'intra', split_axis=1, concat_axis=1, tiled=True)  14.2 us
    all_to_all x2, waiting for transfers between devices, send_home(): lax.all_to_all(summed, 'intra', split_axis=1, concat_axis=1, tiled=True)  9.49 us
  transfers between devices with their start and end apart: 8, of which 8 were waited for; matrix products, arithmetic and copies ran while one was open for 6% of the time, Pallas kernels for 0%

commit v1 on v0

v1 whole, which is shorter than its diff:
```python
import math

import jax
import jax.numpy as jnp
from jax import lax
from jax.sharding import PartitionSpec as P

EGRP = 2


gelu_root = math.sqrt(2.0 / math.pi)
gelu_cubic = 0.044715


def gelu_and_slope(pre_value):
    square = pre_value * pre_value
    argument = gelu_root * (pre_value + gelu_cubic * square * pre_value)
    slope_tanh = jnp.tanh(argument)
    half_up = 0.5 * (1.0 + slope_tanh)
    value = pre_value * half_up
    slope = half_up + 0.5 * pre_value * (1.0 - slope_tanh * slope_tanh) * gelu_root * (
        1.0 + 3.0 * gelu_cubic * square
    )
    return value, slope


def on_device(tokens, expert_ids, slot_ids, keep_mask, gate_prob, out_grad, in_weight, out_weight):
    tok_rows, model_width = tokens.shape
    intra_size = lax.axis_size("intra")
    inter_size = lax.axis_size("inter")
    blocks_ff = inter_size // EGRP
    experts = EGRP * intra_size
    capacity = max(2, tok_rows * 5 // 4 // experts)
    my_group = lax.axis_index("inter") // blocks_ff
    weight_in = in_weight[0, 0]
    weight_out = out_weight[0, 0]
    rows_one = intra_size * capacity
    columns = expert_ids * capacity + slot_ids
    one_hot = (
        (columns[:, None] == jnp.arange(experts * capacity)[None, :]) & (keep_mask[:, None] == 1)
    ).astype(jnp.bfloat16)

    scaled_grad = (gate_prob[:, None] * out_grad.astype(jnp.float32)).astype(jnp.bfloat16)
    both = jnp.concatenate([tokens, scaled_grad], axis=1)
    placed = jnp.einsum("tc,td->cd", one_hot, both, preferred_element_type=jnp.float32).astype(jnp.bfloat16)
    placed = placed.reshape(EGRP, intra_size, capacity, 2 * model_width)
    moved = lax.all_to_all(placed, "intra", split_axis=1, concat_axis=1, tiled=True)
    moved = moved.reshape(1, EGRP, rows_one, 2 * model_width)
    spread = lax.all_gather(moved, "inter", axis=0, tiled=True)
    mine = lax.dynamic_index_in_dim(spread, my_group, axis=1, keepdims=False)
    mine = mine.reshape(inter_size * rows_one, 2 * model_width)
    rows_x, rows_g = mine[:, :model_width], mine[:, model_width:]

    pre_act = jnp.dot(rows_x, weight_in, preferred_element_type=jnp.float32)
    hidden, slope = gelu_and_slope(pre_act)
    hidden = hidden.astype(jnp.bfloat16)
    partial_out = jnp.dot(hidden, weight_out, preferred_element_type=jnp.float32).astype(jnp.bfloat16)
    hidden_grad = jnp.einsum("rd,fd->rf", rows_g, weight_out, preferred_element_type=jnp.float32)
    pre_grad = (hidden_grad * slope).astype(jnp.bfloat16)
    partial_in = jnp.einsum("rf,df->rd", pre_grad, weight_in, preferred_element_type=jnp.float32).astype(jnp.bfloat16)
    partial = jnp.concatenate([partial_out, partial_in], axis=1).reshape(inter_size, 1, rows_one, 2 * model_width)
    which = jnp.arange(EGRP)[None, :, None, None] == my_group
    send = jnp.where(which, partial, jnp.zeros((), jnp.bfloat16))
    summed = lax.psum_scatter(send, "inter", scatter_dimension=0, tiled=True)

    out_weight_grad = jnp.einsum("rf,rd->fd", hidden, rows_g, preferred_element_type=jnp.float32).astype(jnp.bfloat16)
    in_weight_grad = jnp.einsum("rd,rf->df", rows_x, pre_grad, preferred_element_type=jnp.float32).astype(jnp.bfloat16)

    home = lax.all_to_all(
        summed.reshape(EGRP, intra_size, capacity, 2 * model_width), "intra", split_axis=1, concat_axis=1, tiled=True
    )
    home = home.reshape(experts * capacity, 2 * model_width)
    picked = jnp.dot(one_hot, home, preferred_element_type=jnp.float32)
    ffn_tok = picked[:, :model_width]
    expert_out = (gate_prob[:, None] * ffn_tok).astype(jnp.bfloat16)
    gate_grad = jnp.sum(out_grad.astype(jnp.float32) * ffn_tok, axis=1)
    token_grad = picked[:, model_width:].astype(jnp.bfloat16)
    return (
        expert_out,
        gate_grad,
        token_grad,
        in_weight_grad[None, None],
        out_weight_grad[None, None],
    )


def solution(mesh):
    tok = P(("inter", "intra"), None)
    per = P(("inter", "intra"))
    wgt = P("inter", "intra", None, None)
    return jax.shard_map(
        on_device,
        mesh=mesh,
        in_specs=(tok, per, per, per, per, tok, wgt, wgt),
        out_specs=(tok, per, tok, wgt, wgt),
        check_vma=False,
    )
```

time: 395 us -> 252 us (0.64)
  waiting for transfers between devices: 284 us -> 169 us
  starting transfers between devices: 76.3 us -> 14.3 us
  blocking collectives: 0 us -> 19.8 us
  between operations: 0.86 us -> 14.2 us
  matrix products: 19.6 us -> 11.5 us
  other arithmetic: 4.65 us -> 10.7 us
    all_to_all x8 -> x1, waiting for transfers between devices: 284 us -> 4.97 us  [on_device(): lax.all_to_all(summed.reshape(EGRP, intra_size, capacity, 2 * model_width...]
    all_gather x0 -> x1, waiting for transfers between devices: none -> 83.5 us  [on_device(): spread = lax.all_gather(moved, 'inter', axis=0, tiled=True)]
    reduce_scatter x0 -> x1, waiting for transfers between devices: none -> 80.3 us  [on_device(): summed = lax.psum_scatter(send, 'inter', scatter_dimension=0, tiled=True)]
    all_to_all x8 -> x1, starting transfers between devices: 76.3 us -> 14.2 us  [on_device(): lax.all_to_all(summed.reshape(EGRP, intra_size, capacity, 2 * model_width...]
    all_to_all x0 -> x1, blocking collectives: none -> 19.8 us  [on_device(): lax.all_to_all(placed, 'intra', split_axis=1, concat_axis=1, tiled=True)]
    dot_general x10 -> x8, matrix products: 19.6 us -> 11.5 us  [the longest x1 3.39 us: on_device(): jnp.einsum('rd,rf->df', rows_x, pre_grad, preferred_element_type=jnp.floa...]
    select_n x0 -> x1, other arithmetic: none -> 5.02 us  [on_device(): send = jnp.where(which, partial, jnp.zeros((), jnp.bfloat16))]
    concatenate x0 -> x1, local copies, waits for them, and re-layouts: none -> 4.66 us  [on_device(): jnp.concatenate([partial_out, partial_in], axis=1)]
  transfers between devices with their start and end apart: 8 -> 3, of which waited for: 8 -> 3; matrix products, arithmetic and copies ran while one was open for 6% -> 2% of each run, Pallas kernels for 0% -> 0%
where the time goes in v1:
time: 252 us
  waiting for transfers between devices  169 us (67%)
  blocking collectives  19.8 us (8%)
  starting transfers between devices  14.3 us (6%)
  between operations  14.2 us (6%)
  local copies, waits for them, and re-layouts  12.6 us (5%)
  matrix products  11.5 us (5%)
  other arithmetic  10.7 us (4%)
    all_gather x1, waiting for transfers between devices, on_device(): spread = lax.all_gather(moved, 'inter', axis=0, tiled=True)  83.5 us
    reduce_scatter x1, waiting for transfers between devices, on_device(): summed = lax.psum_scatter(send, 'inter', scatter_dimension=0, tiled=True)  80.3 us
    all_to_all x1, blocking collectives, on_device(): lax.all_to_all(placed, 'intra', split_axis=1, concat_axis=1, tiled=True)  19.8 us
    all_to_all x1, starting transfers between devices, on_device(): lax.all_to_all(summed.reshape(EGRP, intra_size, capacity, 2 * model_width...  14.2 us
  transfers between devices with their start and end apart: 3, of which 3 were waited for; matrix products, arithmetic and copies ran while one was open for 2% of the time, Pallas kernels for 0%

profile of v1, /device:TPU:1, one launch (start us, length us, event | category | flops | bytes accessed | tf_op | source)
XLA Modules:
  0.0 251.9 jit_solution(631624559934392678)
XLA Ops:
  7.2 0.0 copy-start
  7.2 0.0 all-gather.2.cloned.1.call-start
  7.2 0.7 broadcast_compare_fusion
  7.9 0.7 multiply_add_fusion.1
  8.6 1.0 fusion.25
  9.6 1.3 convolution_convert_fusion
  11.0 0.1 reshape.37
  11.1 0.3 copy.23
  11.4 19.8 %all_to_all.10 = bf16[2,32,2,1536]{3,2,0,1:T(2,128)(2,1)S(1)} all-to-all(bf16[2,32,2,1536]{3,2,0,1:T(2,128)(2,1)S(1)} %copy.23), channel_id=1, replica_groups=mesh['inter'=16,'intra'=32] {'intra'}, dimensions={1} | all-to-all | bytes 786432 | tf_op jit(solution)/shard_map/all_to_all | solution.py:47
  31.2 0.3 copy.24
  31.5 0.8 copy.25
  32.3 0.0 all-gather.2.cloned.1.call-update
  32.3 0.0 reduce-scatter.2.cloned.1.call-start
  32.4 0.0 copy-start.5
  32.4 83.5 %all-gather.2.cloned.1.call-done = bf16[16,2,64,1536]{3,2,1,0:T(8,128)(2,1)} async-done(((bf16[1,2,64,1536]{3,2,1,0:T(8,128)(2,1)}), bf16[16,2,64,1536]{3,2,1,0:T(8,128)(2,1)}) %all-gather.2.cloned.1.call-update) | async-done | bytes 6291472 | tf_op jit(solution)/shard_map/all_gather | solution.py:49
  115.9 2.2 constant_dynamic-slice_fusion
  118.0 0.0 copy-start.1
  118.1 0.0 copy-done.5
  118.1 1.0 fusion.7
  119.0 0.7 copy-done.1
  119.8 0.0 copy-done
  119.8 0.0 copy-start.6
  119.8 1.6 multiply_convert_fusion
  121.3 0.0 copy-done.6
  121.3 1.2 convolution_convert_fusion.2
  122.5 1.0 convolution_convert_fusion.1
  123.5 1.9 pad_maximum_fusion
  125.5 4.7 %copy.26 = bf16[1024,1536]{1,0:T(8,128)(2,1)} copy(bf16[1024,1536]{0,1:T(8,128)(2,1)} %pad_maximum_fusion) | data formatting | bytes 6291456 | tf_op jit(solution)/shard_map/concatenate | solution.py:61
  130.1 5.0 %broadcast_select_fusion = bf16[16,2,64,1536]{3,2,1,0:T(8,128)(2,1)} fusion(pred[2]{0:T(512)(128)(4,1)S(1)} %iota_compare_fusion.1, bf16[16,64,1536]{2,1,0:T(8,128)(2,1)} %bitcast.21), kind=kLoop, calls=%fused_computation | loop fusion | flops 3145728 | bytes 9437186 | tf_op jit(solution)/shard_map/jit(_where)/select_n | solution.py:63
  135.1 0.0 reduce-scatter.2.cloned.1.call-update
  135.2 80.3 %reduce-scatter.2.cloned.1.call-done = bf16[1,2,64,1536]{3,2,1,0:T(8,128)(2,1)} async-done(((bf16[16,2,64,1536]{3,2,1,0:T(8,128)(2,1)}), bf16[1,2,64,1536]{3,2,1,0:T(8,128)(2,1)}) %reduce-scatter.2.cloned.1.call-update) | async-done | bytes 393232 | tf_op jit(solution)/shard_map/reduce_scatter | solution.py:64
  215.5 1.4 copy.27
  216.9 1.0 copy.28
  217.9 14.2 %all-to-all-start.1 = ((bf16[2,32,2,1536]{3,2,0,1:T(2,128)(2,1)}), bf16[2,32,2,1536]{3,2,0,1:T(2,128)(2,1)S(1)}, u32[]{:S(2)}, u32[]{:S(2)}) async-start(bf16[2,32,2,1536]{3,2,0,1:T(2,128)(2,1)} %copy.28), calls=%async_computation.2 | async-start | bytes 786432 | tf_op jit(solution)/shard_map/all_to_all | solution.py:69
  232.1 0.0 copy-start.2
  232.1 0.0 copy-start.7
  232.1 3.4 %fusion.18 = bf16[1,1,768,384]{3,2,1,0:T(8,128)(2,1)} fusion(bf16[1024,384]{1,0:T(8,128)(2,1)S(1)} %multiply_convert_fusion, bf16[1024,1536]{1,0:T(8,128)(2,1)} %bitcast.24), kind=kOutput, calls=%fused_computation.21 | convolution fusion | flops 604274688 | bytes 2949120 | tf_op jit(solution)/shard_map/rd,rf->df/dot_general | solution.py:67
  235.5 0.0 copy-done.2
  235.5 0.0 copy-done.7
  235.5 1.8 fusion.15
  237.3 5.0 %all-to-all-done.1 = bf16[2,32,2,1536]{3,2,0,1:T(2,128)(2,1)S(1)} async-done(((bf16[2,32,2,1536]{3,2,0,1:T(2,128)(2,1)}), bf16[2,32,2,1536]{3,2,0,1:T(2,128)(2,1)S(1)}, u32[]{:S(2)}, u32[]{:S(2)}) %all-to-all-start.1) | async-done | bytes 393248 | tf_op jit(solution)/shard_map/all_to_all | solution.py:69
  242.3 0.3 copy.29
  242.6 0.1 reshape.41
  242.7 0.3 fusion.31
  243.0 0.7 slice.40
  243.7 0.0 copy-done.3
  243.7 0.0 copy-done.4
  243.7 1.3 fusion.26
  (3 shorter events, 0.0 us)
Async XLA Ops:
  7.2 112.6 %copy-start = (bf16[1,1,384,768]{3,2,1,0:T(8,128)(2,1)S(1)}, bf16[1,1,384,768]{3,2,1,0:T(8,128)(2,1)}, u32[]{:S(2)}) copy-start(bf16[1,1,384,768]{3,2,1,0:T(8,128)(2,1)} %param.15) | copy-start | bytes 1769476
  7.2 108.7 %all-gather.2.cloned.1.call-start = ((), (), s32[]{:S(2)}) async-start(), calls=%async_computation.3 | async-start | bytes 6684672 | tf_op jit(solution)/shard_map/all_gather | solution.py:49
  32.3 183.1 %reduce-scatter.2.cloned.1.call-start = ((), (), s32[]{:S(2)}) async-start(), calls=%async_computation.4 | async-start | bytes 6684672 | tf_op jit(solution)/shard_map/reduce_scatter | solution.py:64
  32.4 85.7 %copy-start.5 = (bf16[1,1,768,384]{3,2,1,0:T(8,128)(2,1)S(1)}, bf16[1,1,768,384]{3,2,1,0:T(8,128)(2,1)}, u32[]{:S(2)}) copy-start(bf16[1,1,768,384]{3,2,1,0:T(8,128)(2,1)} %param.14) | copy-start | bytes 1769476
  118.0 1.7 copy-start.1
  119.8 1.6 copy-start.6
  217.9 24.4 %all-to-all-start.1 = ((bf16[2,32,2,1536]{3,2,0,1:T(2,128)(2,1)}), bf16[2,32,2,1536]{3,2,0,1:T(2,128)(2,1)S(1)}, u32[]{:S(2)}, u32[]{:S(2)}) async-start(bf16[2,32,2,1536]{3,2,0,1:T(2,128)(2,1)} %copy.28), calls=%async_computation.2 | async-start | bytes 786432 | tf_op jit(solution)/shard_map/all_to_all | solution.py:69
  232.1 3.4 %copy-start.2 = (bf16[16,1,64,1536]{3,2,1,0:T(8,128)(2,1)S(1)}, bf16[16,1,64,1536]{3,2,1,0:T(8,128)(2,1)}, u32[]{:S(2)}) copy-start(bf16[16,1,64,1536]{3,2,1,0:T(8,128)(2,1)} %copy-done.1) | copy-start | bytes 9437188
  232.1 3.4 %copy-start.7 = (f32[1024,384]{1,0:T(8,128)S(1)}, f32[1024,384]{1,0:T(8,128)}, u32[]{:S(2)}) copy-start(f32[1024,384]{1,0:T(8,128)} %copy-done.6) | copy-start | bytes 4718596
  237.3 6.4 %copy-start.3 = (bf16[128,768]{1,0:T(8,128)(2,1)S(1)}, bf16[128,768]{1,0:T(8,128)(2,1)}, u32[]{:S(2)}) copy-start(bf16[128,768]{1,0:T(8,128)(2,1)} %param.13) | copy-start | bytes 589828
  237.3 6.4 %copy-start.4 = (f32[128]{0:T(128)S(1)}, f32[128]{0:T(128)}, u32[]{:S(2)}) copy-start(f32[128]{0:T(128)} %param.12) | copy-start | bytes 1540
Sparse Core Ops, SparseCore 0:
  32.4 83.3 all-gather.1
  135.3 80.1 reduce-scatter.1

commit v2 on v1

v2 whole, which is shorter than its diff:
```python
import functools
import math

import jax
import jax.numpy as jnp
from jax import lax
from jax.experimental import pallas as pl
from jax.experimental.pallas import tpu as pltpu
from jax.sharding import PartitionSpec as P

EGRP = 2
CAP = 2
KINDS = 2
TILE = EGRP * KINDS * CAP
VMEM_BYTES = 48 * 1024 * 1024

gelu_root = math.sqrt(2.0 / math.pi)
gelu_cubic = 0.044715


def gelu_and_slope(pre_value):
    square = pre_value * pre_value
    argument = gelu_root * (pre_value + gelu_cubic * square * pre_value)
    slope_tanh = jnp.tanh(argument)
    half_up = 0.5 * (1.0 + slope_tanh)
    value = pre_value * half_up
    slope = half_up + 0.5 * pre_value * (1.0 - slope_tanh * slope_tanh) * gelu_root * (
        1.0 + 3.0 * gelu_cubic * square
    )
    return value, slope


def dot(left, right, dims=((1,), (0,))):
    return lax.dot_general(left, right, (dims, ((), ())), preferred_element_type=jnp.float32)


def slot_row(experts, slots, keep, intra_size):
    group = (experts >= intra_size).astype(jnp.int32)
    row = (experts - group * intra_size) * TILE + group * (KINDS * CAP) + slots
    return jnp.where(keep == 1, row, -TILE)


def as_column(row):
    count = row.shape[1]
    shape = (count, count)
    diagonal = lax.broadcasted_iota(jnp.int32, shape, 0) == lax.broadcasted_iota(jnp.int32, shape, 1)
    return jnp.sum(jnp.where(diagonal, row, 0.0), axis=1, keepdims=True)


def as_row(column):
    count = column.shape[0]
    shape = (count, count)
    diagonal = lax.broadcasted_iota(jnp.int32, shape, 0) == lax.broadcasted_iota(jnp.int32, shape, 1)
    return jnp.sum(jnp.where(diagonal, column, 0.0), axis=0, keepdims=True)


def place_kernel(intra_size, tokens, experts, slots, keep, gate, out_grad, send):
    count = tokens.shape[0]
    row = slot_row(experts[...], slots[...], keep[...], intra_size)
    scaled = (as_column(gate[...]) * out_grad[...].astype(jnp.float32)).astype(jnp.bfloat16)
    at = lax.broadcasted_iota(jnp.int32, (send.shape[0], count), 0)
    hot_x = (at == row).astype(jnp.bfloat16)
    hot_g = (at == row + CAP).astype(jnp.bfloat16)
    send[...] = (dot(hot_x, tokens[...]) + dot(hot_g, scaled)).astype(jnp.bfloat16)


def pick_kernel(intra_size, home, experts, slots, keep, gate, out_grad, expert_out, gate_grad, token_grad):
    count = out_grad.shape[0]
    row = slot_row(experts[...], slots[...], keep[...], intra_size)
    row = as_column(row.astype(jnp.float32)).astype(jnp.int32)
    at = lax.broadcasted_iota(jnp.int32, (count, home.shape[0]), 1)
    ffn_tok = dot((at == row).astype(jnp.bfloat16), home[...])
    expert_out[...] = (as_column(gate[...]) * ffn_tok).astype(jnp.bfloat16)
    gate_grad[...] = as_row(jnp.sum(out_grad[...].astype(jnp.float32) * ffn_tok, axis=1, keepdims=True))
    token_grad[...] = dot((at == row + CAP).astype(jnp.bfloat16), home[...]).astype(jnp.bfloat16)


def expert_kernel(group_ref, rows, weight_in, weight_out, send, rows_x, rows_g, hidden, pre_grad):
    sources, wide, _ = rows.shape
    narrow = wide // EGRP
    half = narrow // KINDS
    first = group_ref[0] * (KINDS * CAP)

    def place_of(index):
        kind = (index >= half).astype(jnp.int32)
        within = index - kind * half
        return (within >> 1) * TILE + first + kind * CAP + (within & 1)

    shape = (narrow, wide)
    take = (
        lax.broadcasted_iota(jnp.int32, shape, 1) == place_of(lax.broadcasted_iota(jnp.int32, shape, 0))
    ).astype(jnp.bfloat16)
    shape = (wide, narrow)
    put = (
        lax.broadcasted_iota(jnp.int32, shape, 0) == place_of(lax.broadcasted_iota(jnp.int32, shape, 1))
    ).astype(jnp.bfloat16)
    for s in range(sources):
        taken = dot(take, rows[s]).astype(jnp.bfloat16)
        rows_x[pl.ds(s * half, half), :] = taken[:half]
        rows_g[pl.ds(s * half, half), :] = taken[half:]
    pre_act = dot(rows_x[...], weight_in[...])
    hidden_grad = dot(rows_g[...], weight_out[...], ((1,), (1,)))
    value, slope = gelu_and_slope(pre_act)
    hidden[...] = value.astype(jnp.bfloat16)
    pre_grad[...] = (hidden_grad * slope).astype(jnp.bfloat16)
    part_out = dot(hidden[...], weight_out[...]).astype(jnp.bfloat16)
    part_in = dot(pre_grad[...], weight_in[...], ((1,), (1,))).astype(jnp.bfloat16)
    for s in range(sources):
        both = jnp.concatenate([part_out[s * half : (s + 1) * half], part_in[s * half : (s + 1) * half]], axis=0)
        send[s] = dot(put, both).astype(jnp.bfloat16)


def on_device(tokens, expert_ids, slot_ids, keep_mask, gate_prob, out_grad, in_weight, out_weight):
    tok_rows, width = tokens.shape
    intra_size = lax.axis_size("intra")
    inter_size = lax.axis_size("inter")
    blocks_ff = inter_size // EGRP
    group = (lax.axis_index("inter") // blocks_ff).astype(jnp.int32).reshape(1)
    weight_in = in_weight[0, 0]
    weight_out = out_weight[0, 0]
    hidden_units = weight_in.shape[1]
    wide = intra_size * TILE
    params = pltpu.CompilerParams(vmem_limit_bytes=VMEM_BYTES)
    routing = (expert_ids[None], slot_ids[None], keep_mask[None], gate_prob[None])

    placed = pl.pallas_call(
        functools.partial(place_kernel, intra_size),
        out_shape=jax.ShapeDtypeStruct((wide, width), jnp.bfloat16),
        compiler_params=params,
        name="place",
    )(tokens, *routing, out_grad)
    moved = lax.all_to_all(placed.reshape(intra_size, TILE, width), "intra", 0, 0, tiled=True)
    spread = lax.all_gather(moved.reshape(1, wide, width), "inter", axis=0, tiled=True)

    step = 4
    rows_step = step * wide // (EGRP * KINDS)
    rows_all = inter_size * wide // (EGRP * KINDS)
    whole = lambda i, *_: (0, 0)
    by_row = lambda i, *_: (i, 0)
    send, rows_x, rows_g, hidden, pre_grad = pl.pallas_call(
        expert_kernel,
        grid_spec=pltpu.PrefetchScalarGridSpec(
            num_scalar_prefetch=1,
            grid=(inter_size // step,),
            in_specs=[
                pl.BlockSpec((step, wide, width), lambda i, *_: (i, 0, 0)),
                pl.BlockSpec((width, hidden_units), whole),
                pl.BlockSpec((hidden_units, width), whole),
            ],
            out_specs=[
                pl.BlockSpec((step, wide, width), lambda i, *_: (i, 0, 0)),
                pl.BlockSpec((rows_step, width), by_row),
                pl.BlockSpec((rows_step, width), by_row),
                pl.BlockSpec((rows_step, hidden_units), by_row),
                pl.BlockSpec((rows_step, hidden_units), by_row),
            ],
        ),
        out_shape=[
            jax.ShapeDtypeStruct((inter_size, wide, width), jnp.bfloat16),
            jax.ShapeDtypeStruct((rows_all, width), jnp.bfloat16),
            jax.ShapeDtypeStruct((rows_all, width), jnp.bfloat16),
            jax.ShapeDtypeStruct((rows_all, hidden_units), jnp.bfloat16),
            jax.ShapeDtypeStruct((rows_all, hidden_units), jnp.bfloat16),
        ],
        compiler_params=params,
        name="expert",
    )(group, spread, weight_in, weight_out)
    summed = lax.psum_scatter(send, "inter", scatter_dimension=0, tiled=True)

    out_weight_grad = dot(hidden, rows_g, ((0,), (0,))).astype(jnp.bfloat16)
    in_weight_grad = dot(rows_x, pre_grad, ((0,), (0,))).astype(jnp.bfloat16)
    summed, out_weight_grad, in_weight_grad = lax.optimization_barrier((summed, out_weight_grad, in_weight_grad))

    home = lax.all_to_all(summed.reshape(intra_size, TILE, width), "intra", 0, 0, tiled=True)
    expert_out, gate_grad, token_grad = pl.pallas_call(
        functools.partial(pick_kernel, intra_size),
        out_shape=[
            jax.ShapeDtypeStruct((tok_rows, width), jnp.bfloat16),
            jax.ShapeDtypeStruct((1, tok_rows), jnp.float32),
            jax.ShapeDtypeStruct((tok_rows, width), jnp.bfloat16),
        ],
        compiler_params=params,
        name="pick",
    )(home.reshape(wide, width), *routing, out_grad)
    return (
        expert_out,
        gate_grad.reshape(tok_rows),
        token_grad,
        in_weight_grad[None, None],
        out_weight_grad[None, None],
    )


def solution(mesh):
    tok = P(("inter", "intra"), None)
    per = P(("inter", "intra"))
    wgt = P("inter", "intra", None, None)
    return jax.shard_map(
        on_device,
        mesh=mesh,
        in_specs=(tok, per, per, per, per, tok, wgt, wgt),
        out_specs=(tok, per, tok, wgt, wgt),
        check_vma=False,
    )
```

time: 252 us -> 241 us (0.956)
  blocking collectives: 19.8 us -> 44.8 us
  starting transfers between devices: 14.3 us -> 0.08 us
  Pallas kernels: 0 us -> 11.3 us
  other arithmetic: 10.7 us -> 0 us
  waiting for transfers between devices: 169 us -> 160 us
  matrix products: 11.5 us -> 3.45 us
  local copies, waits for them, and re-layouts: 12.6 us -> 6.62 us
    all_to_all x1 -> x2, blocking collectives: 19.8 us -> 44.8 us  [the longest x1 24.3 us: on_device(): lax.all_to_all(summed.reshape(intra_size, TILE, width), 'intra', 0, 0, ti...]
    all_to_all x1 -> x0, starting transfers between devices: 14.2 us -> none  [on_device(): lax.all_to_all(summed.reshape(EGRP, intra_size, capacity, 2 * model_width...]
    pallas_call x0 -> x3, Pallas kernels: none -> 11.3 us  [the longest x1 9.76 us: on_device(): pl.pallas_call(expert_kernel, grid_spec=pltpu.PrefetchScalarGridSpec(num_...]
    dot_general x8 -> x2, matrix products: 11.5 us -> 3.45 us  [dot(): lax.dot_general(left, right, (dims, ((), ())), preferred_element_type=jnp...]
    unnamed x16 -> x34, local copies, waits for them, and re-layouts: 0.75 us -> 6.62 us
    select_n x1 -> x0, other arithmetic: 5.02 us -> none  [on_device(): send = jnp.where(which, partial, jnp.zeros((), jnp.bfloat16))]
    all_to_all x1 -> x0, waiting for transfers between devices: 4.97 us -> none  [on_device(): lax.all_to_all(summed.reshape(EGRP, intra_size, capacity, 2 * model_width...]
    concatenate x1 -> x0, local copies, waits for them, and re-layouts: 4.66 us -> none  [on_device(): jnp.concatenate([partial_out, partial_in], axis=1)]
  transfers between devices with their start and end apart: 3 -> 2, of which waited for: 3 -> 2; matrix products, arithmetic and copies ran while one was open for 2% -> 1% of each run, Pallas kernels for 0% -> 0%
where the time goes in v2:
time: 241 us; the launch traced here: 240 us
  waiting for transfers between devices  160 us (66%)
  blocking collectives  44.8 us (19%)
  between operations  14.1 us (6%)
  Pallas kernels  11.3 us (5%)
  local copies, waits for them, and re-layouts  6.62 us (3%)
  matrix products  3.45 us (1%)
    all_gather x1, waiting for transfers between devices, on_device(): lax.all_gather(moved.reshape(1, wide, width), 'inter', axis=0, tiled=True)  82.9 us
    reduce_scatter x1, waiting for transfers between devices, on_device(): summed = lax.psum_scatter(send, 'inter', scatter_dimension=0, tiled=True)  76.8 us
    all_to_all x1, blocking collectives, on_device(): lax.all_to_all(summed.reshape(intra_size, TILE, width), 'intra', 0, 0, ti...  24.3 us
    all_to_all x1, blocking collectives, on_device(): lax.all_to_all(placed.reshape(intra_size, TILE, width), 'intra', 0, 0, ti...  20.5 us
    pallas_call x1, Pallas kernels, on_device(): pl.pallas_call(expert_kernel, grid_spec=pltpu.PrefetchScalarGridSpec(num_...  9.76 us
    unnamed x34, local copies, waits for them, and re-layouts  6.62 us
  transfers between devices with their start and end apart: 2, of which 2 were waited for; matrix products, arithmetic and copies ran while one was open for 1% of the time, Pallas kernels for 0%

profile of v2, /device:TPU:1, one launch (start us, length us, event | category | flops | bytes accessed | tf_op | source)
XLA Modules:
  0.0 240.2 jit_solution(11173879864543505362)
XLA Ops:
  7.2 0.0 all-gather.2.cloned.1.call-start
  7.2 0.0 copy-start
  7.2 0.9 copy-done
  8.1 0.0 copy-start.4
  8.1 0.9 copy-done.4
  9.1 0.0 copy-start.5
  9.1 0.7 copy-done.5
  9.7 0.0 copy-start.7
  9.7 0.7 copy-done.7
  10.4 0.0 copy-start.9
  10.4 0.7 copy-done.9
  11.0 0.0 copy-start.11
  11.0 0.7 copy-done.11
  11.7 0.0 copy-start.2
  11.7 0.0 copy-start.3
  11.7 0.4 place.1
  12.1 20.5 %all_to_all.10 = bf16[32,8,768]{2,1,0:T(8,128)(2,1)} all-to-all(bf16[32,8,768]{2,1,0:T(8,128)(2,1)S(1)} %bitcast.19), channel_id=1, replica_groups=mesh['inter'=16,'intra'=32] {'intra'}, dimensions={0} | all-to-all | bytes 786432 | tf_op jit(solution)/shard_map/all_to_all | solution.py:132
  32.6 0.0 all-gather.2.cloned.1.call-update
  32.6 0.0 reduce-scatter.2.cloned.1.call-start
  32.7 82.9 %all-gather.2.cloned.1.call-done.rows = bf16[16,256,768]{2,1,0:T(8,128)(2,1)} async-done(((bf16[1,256,768]{2,1,0:T(8,128)(2,1)}), bf16[16,256,768]{2,1,0:T(8,128)(2,1)}) %all-gather.2.cloned.1.call-update) | async-done | bytes 6291472 | tf_op jit(solution)/shard_map/all_gather | solution.py:133
  115.6 0.0 copy-done.2
  115.6 0.0 copy-done.3
  115.6 9.8 %expert.1 = (bf16[16,256,768]{2,1,0:T(8,128)(2,1)}, bf16[1024,768]{1,0:T(8,128)(2,1)S(1)}, bf16[1024,768]{1,0:T(8,128)(2,1)S(1)}, bf16[1024,384]{1,0:T(8,128)(2,1)S(1)}, bf16[1024,384]{1,0:T(8,128)(2,1)S(1)}) custom-call(s32[1]{0:T(128)} %bitcast.group_ref, bf16[16,256,768]{2,1,0:T(8,128)(2,1)} %all-gather.2.cloned.1.call-done.rows, ...), custom_call_target="tpu_custom_call" | custom-call | tf_op jit(solution)/shard_map/expert/pallas_call | solution.py:140
  125.4 0.0 copy-start.13
  125.4 1.2 copy-done.13
  126.5 0.0 copy-start.15
  126.5 0.9 copy-done.15
  127.5 0.0 reduce-scatter.2.cloned.1.call-update
  127.5 0.0 copy-start.14
  127.5 0.0 copy-start.16
  127.5 1.6 convolution_convert_fusion.1
  129.2 0.0 copy-done.14
  129.2 0.0 copy-done.16
  129.2 0.0 copy-start.1
  129.2 0.0 copy-start.6
  129.2 0.0 copy-start.8
  129.2 0.0 copy-start.10
  129.2 0.0 copy-start.12
  129.2 1.8 convolution_convert_fusion
  131.0 76.8 %reduce-scatter.2.cloned.1.call-done = bf16[1,256,768]{2,1,0:T(8,128)(2,1)} async-done(((bf16[16,256,768]{2,1,0:T(8,128)(2,1)}), bf16[1,256,768]{2,1,0:T(8,128)(2,1)}) %reduce-scatter.2.cloned.1.call-update) | async-done | bytes 393232 | tf_op jit(solution)/shard_map/reduce_scatter | solution.py:168
  207.8 24.3 %all_to_all.11 = bf16[32,8,768]{2,1,0:T(8,128)(2,1)S(1)} all-to-all(bf16[32,8,768]{2,1,0:T(8,128)(2,1)} %bitcast.32), channel_id=1, replica_groups=mesh['inter'=16,'intra'=32] {'intra'}, dimensions={0} | all-to-all | bytes 786432 | tf_op jit(solution)/shard_map/all_to_all | solution.py:174
  232.2 0.0 copy-done.1
  232.2 0.0 copy-done.6
  232.2 0.0 copy-done.8
  232.2 0.0 copy-done.10
  232.2 0.0 copy-done.12
  232.2 1.1 pick.1
Async XLA Ops:
  7.2 108.5 %all-gather.2.cloned.1.call-start = ((), (), s32[]{:S(2)}) async-start(), calls=%async_computation.3 | async-start | bytes 6684672 | tf_op jit(solution)/shard_map/all_gather | solution.py:133
  7.2 0.9 copy-start
  8.1 0.9 copy-start.4
  9.1 0.7 copy-start.5
  9.7 0.7 copy-start.7
  10.4 0.7 copy-start.9
  11.0 0.7 copy-start.11
  11.7 103.9 %copy-start.2 = (bf16[1,1,768,384]{3,2,1,0:T(8,128)(2,1)S(1)}, bf16[1,1,768,384]{3,2,1,0:T(8,128)(2,1)}, u32[]{:S(2)}) copy-start(bf16[1,1,768,384]{3,2,1,0:T(8,128)(2,1)} %param.14) | copy-start | bytes 1769476
  11.7 103.9 %copy-start.3 = (bf16[1,1,384,768]{3,2,1,0:T(8,128)(2,1)S(1)}, bf16[1,1,384,768]{3,2,1,0:T(8,128)(2,1)}, u32[]{:S(2)}) copy-start(bf16[1,1,384,768]{3,2,1,0:T(8,128)(2,1)} %param.15) | copy-start | bytes 1769476
  32.6 175.2 %reduce-scatter.2.cloned.1.call-start = ((), (), s32[]{:S(2)}) async-start(), calls=%async_computation.4 | async-start | bytes 6684672 | tf_op jit(solution)/shard_map/reduce_scatter | solution.py:168
  125.4 1.2 copy-start.13
  126.5 0.9 copy-start.15
  127.5 1.7 copy-start.14
  127.5 1.6 copy-start.16
  129.2 103.0 %copy-start.1 = (bf16[128,768]{1,0:T(8,128)(2,1)S(1)}, bf16[128,768]{1,0:T(8,128)(2,1)}, u32[]{:S(2)}) copy-start(bf16[128,768]{1,0:T(8,128)(2,1)} %out_grad.3) | copy-start | bytes 589828
  129.2 103.0 %copy-start.6 = (s32[128]{0:T(128)S(1)}, s32[128]{0:T(128)}, u32[]{:S(2)}) copy-start(s32[128]{0:T(128)} %param.9) | copy-start | bytes 1540
  129.2 103.0 %copy-start.8 = (s32[128]{0:T(128)S(1)}, s32[128]{0:T(128)}, u32[]{:S(2)}) copy-start(s32[128]{0:T(128)} %param.10) | copy-start | bytes 1540
  129.2 103.0 %copy-start.10 = (s32[128]{0:T(128)S(1)}, s32[128]{0:T(128)}, u32[]{:S(2)}) copy-start(s32[128]{0:T(128)} %param.11) | copy-start | bytes 1540
  129.2 103.0 %copy-start.12 = (f32[128]{0:T(128)S(1)}, f32[128]{0:T(128)}, u32[]{:S(2)}) copy-start(f32[128]{0:T(128)} %param.12) | copy-start | bytes 1540
Sparse Core Ops, SparseCore 0:
  32.8 82.8 all-gather.1
  127.6 80.1 reduce-scatter.1

commit v3 on v2

--- a/solution.py
+++ b/solution.py
@@ -12,7 +12,7 @@
 CAP = 2
 KINDS = 2
 TILE = EGRP * KINDS * CAP
-VMEM_BYTES = 48 * 1024 * 1024
+VMEM_BYTES = 60 * 1024 * 1024
 
 gelu_root = math.sqrt(2.0 / math.pi)
 gelu_cubic = 0.044715
@@ -75,25 +75,21 @@
     token_grad[...] = dot((at == row + CAP).astype(jnp.bfloat16), home[...]).astype(jnp.bfloat16)
 
 
-def expert_kernel(group_ref, rows, weight_in, weight_out, send, rows_x, rows_g, hidden, pre_grad):
+def row_places(narrow, wide, first, transposed):
+    half = narrow // KINDS
+    shape = (wide, narrow) if transposed else (narrow, wide)
+    index = lax.broadcasted_iota(jnp.int32, shape, 1 if transposed else 0)
+    at = lax.broadcasted_iota(jnp.int32, shape, 0 if transposed else 1)
+    kind = (index >= half).astype(jnp.int32)
+    within = index - kind * half
+    return (at == (within >> 1) * TILE + first + kind * CAP + (within & 1)).astype(jnp.bfloat16)
+
+
+def forward_rows(group_ref, rows, weight_in, weight_out, rows_x, rows_g):
     sources, wide, _ = rows.shape
     narrow = wide // EGRP
     half = narrow // KINDS
-    first = group_ref[0] * (KINDS * CAP)
-
-    def place_of(index):
-        kind = (index >= half).astype(jnp.int32)
-        within = index - kind * half
-        return (within >> 1) * TILE + first + kind * CAP + (within & 1)
-
-    shape = (narrow, wide)
-    take = (
-        lax.broadcasted_iota(jnp.int32, shape, 1) == place_of(lax.broadcasted_iota(jnp.int32, shape, 0))
-    ).astype(jnp.bfloat16)
-    shape = (wide, narrow)
-    put = (
-        lax.broadcasted_iota(jnp.int32, shape, 0) == place_of(lax.broadcasted_iota(jnp.int32, shape, 1))
-    ).astype(jnp.bfloat16)
+    take = row_places(narrow, wide, group_ref[0] * (KINDS * CAP), False)
     for s in range(sources):
         taken = dot(take, rows[s]).astype(jnp.bfloat16)
         rows_x[pl.ds(s * half, half), :] = taken[:half]
@@ -101,13 +97,37 @@
     pre_act = dot(rows_x[...], weight_in[...])
     hidden_grad = dot(rows_g[...], weight_out[...], ((1,), (1,)))
     value, slope = gelu_and_slope(pre_act)
-    hidden[...] = value.astype(jnp.bfloat16)
-    pre_grad[...] = (hidden_grad * slope).astype(jnp.bfloat16)
-    part_out = dot(hidden[...], weight_out[...]).astype(jnp.bfloat16)
-    part_in = dot(pre_grad[...], weight_in[...], ((1,), (1,))).astype(jnp.bfloat16)
+    return value.astype(jnp.bfloat16), (hidden_grad * slope).astype(jnp.bfloat16)
+
+
+def expert_kernel(group_ref, rows, weight_in, weight_out, send, rows_x, rows_g):
+    sources, wide, _ = rows.shape
+    narrow = wide // EGRP
+    half = narrow // KINDS
+    hidden, pre_grad = forward_rows(group_ref, rows, weight_in, weight_out, rows_x, rows_g)
+    part_out = dot(hidden, weight_out[...]).astype(jnp.bfloat16)
+    part_in = dot(pre_grad, weight_in[...], ((1,), (1,))).astype(jnp.bfloat16)
+    put = row_places(narrow, wide, group_ref[0] * (KINDS * CAP), True)
     for s in range(sources):
         both = jnp.concatenate([part_out[s * half : (s + 1) * half], part_in[s * half : (s + 1) * half]], axis=0)
         send[s] = dot(put, both).astype(jnp.bfloat16)
+
+
+def weights_kernel(group_ref, rows, weight_in, weight_out, grad_in, grad_out, rows_x, rows_g, sum_in, sum_out):
+    hidden, pre_grad = forward_rows(group_ref, rows, weight_in, weight_out, rows_x, rows_g)
+
+    @pl.when(pl.program_id(0) == 0)
+    def _():
+        sum_in[...] = jnp.zeros_like(sum_in)
+        sum_out[...] = jnp.zeros_like(sum_out)
+
+    sum_in[...] += dot(rows_x[...], pre_grad, ((0,), (0,)))
+    sum_out[...] += dot(hidden, rows_g[...], ((0,), (0,)))
+
+    @pl.when(pl.program_id(0) == pl.num_programs(0) - 1)
+    def _():
+        grad_in[...] = sum_in[...].astype(grad_in.dtype)
+        grad_out[...] = sum_out[...].astype(grad_out.dtype)
 
 
 def on_device(tokens, expert_ids, slot_ids, keep_mask, gate_prob, out_grad, in_weight, out_weight):
@@ -134,41 +154,38 @@
 
     step = 4
     rows_step = step * wide // (EGRP * KINDS)
-    rows_all = inter_size * wide // (EGRP * KINDS)
     whole = lambda i, *_: (0, 0)
-    by_row = lambda i, *_: (i, 0)
-    send, rows_x, rows_g, hidden, pre_grad = pl.pallas_call(
-        expert_kernel,
-        grid_spec=pltpu.PrefetchScalarGridSpec(
-            num_scalar_prefetch=1,
-            grid=(inter_size // step,),
-            in_specs=[
-                pl.BlockSpec((step, wide, width), lambda i, *_: (i, 0, 0)),
-                pl.BlockSpec((width, hidden_units), whole),
-                pl.BlockSpec((hidden_units, width), whole),
-            ],
-            out_specs=[
-                pl.BlockSpec((step, wide, width), lambda i, *_: (i, 0, 0)),
-                pl.BlockSpec((rows_step, width), by_row),
-                pl.BlockSpec((rows_step, width), by_row),
-                pl.BlockSpec((rows_step, hidden_units), by_row),
-                pl.BlockSpec((rows_step, hidden_units), by_row),
-            ],
-        ),
-        out_shape=[
-            jax.ShapeDtypeStruct((inter_size, wide, width), jnp.bfloat16),
-            jax.ShapeDtypeStruct((rows_all, width), jnp.bfloat16),
-            jax.ShapeDtypeStruct((rows_all, width), jnp.bfloat16),
-            jax.ShapeDtypeStruct((rows_all, hidden_units), jnp.bfloat16),
-            jax.ShapeDtypeStruct((rows_all, hidden_units), jnp.bfloat16),
-        ],
-        compiler_params=params,
-        name="expert",
-    )(group, spread, weight_in, weight_out)
+    by_plane = pl.BlockSpec((step, wide, width), lambda i, *_: (i, 0, 0))
+    in_block = pl.BlockSpec((width, hidden_units), whole)
+    out_block = pl.BlockSpec((hidden_units, width), whole)
+    row_scratch = [pltpu.VMEM((rows_step, width), jnp.bfloat16)] * 2
+
+    def over_planes(kernel, name, out_specs, out_shape, scratch):
+        return pl.pallas_call(
+            kernel,
+            grid_spec=pltpu.PrefetchScalarGridSpec(
+                num_scalar_prefetch=1,
+                grid=(inter_size // step,),
+                in_specs=[by_plane, in_block, out_block],
+                out_specs=out_specs,
+                scratch_shapes=row_scratch + scratch,
+            ),
+            out_shape=out_shape,
+            compiler_params=params,
+            name=name,
+        )(group, spread, weight_in, weight_out)
+
+    send = over_planes(
+        expert_kernel, "expert", by_plane, jax.ShapeDtypeStruct((inter_size, wide, width), jnp.bfloat16), []
+    )
     summed = lax.psum_scatter(send, "inter", scatter_dimension=0, tiled=True)
-
-    out_weight_grad = dot(hidden, rows_g, ((0,), (0,))).astype(jnp.bfloat16)
-    in_weight_grad = dot(rows_x, pre_grad, ((0,), (0,))).astype(jnp.bfloat16)
+    in_weight_grad, out_weight_grad = over_planes(
+        weights_kernel,
+        "weight_grads",
+        [in_block, out_block],
+        [jax.ShapeDtypeStruct(w.shape, jnp.bfloat16) for w in (weight_in, weight_out)],
+        [pltpu.VMEM(w.shape, jnp.float32) for w in (weight_in, weight_out)],
+    )
     summed, out_weight_grad, in_weight_grad = lax.optimization_barrier((summed, out_weight_grad, in_weight_grad))
 
     home = lax.all_to_all(summed.reshape(intra_size, TILE, width), "intra", 0, 0, tiled=True)

time: 241 us -> 237 us (0.983)
  Pallas kernels: 11.3 us -> 23.1 us
  local copies, waits for them, and re-layouts: 6.62 us -> 0 us
  waiting for transfers between devices: 160 us -> 154 us
  matrix products: 3.45 us -> 0 us
    pallas_call x1 -> x2, Pallas kernels: 9.76 us -> 18.6 us  [over_planes(): pl.pallas_call(kernel, grid_spec=pltpu.PrefetchScalarGridSpec(num_scalar_...]
    unnamed x34 -> x0, local copies, waits for them, and re-layouts: 6.62 us -> none
    reduce_scatter x1, waiting for transfers between devices: 76.8 us -> 71.8 us  [on_device(): summed = lax.psum_scatter(send, 'inter', scatter_dimension=0, tiled=True)]
    dot_general x2 -> x0, matrix products: 3.45 us -> none  [dot(): lax.dot_general(left, right, (dims, ((), ())), preferred_element_type=jnp...]
  transfers between devices with their start and end apart: 2 -> 2, of which waited for: 2 -> 2; matrix products, arithmetic and copies ran while one was open for 1% -> 0% of each run, Pallas kernels for 0% -> 4%
where the time goes in v3:
time: 237 us
  waiting for transfers between devices  154 us (65%)
  blocking collectives  45.7 us (19%)
  Pallas kernels  23.1 us (10%)
  between operations  14.1 us (6%)
    all_gather x1, waiting for transfers between devices, on_device(): lax.all_gather(moved.reshape(1, wide, width), 'inter', axis=0, tiled=True)  82.2 us
    reduce_scatter x1, waiting for transfers between devices, on_device(): summed = lax.psum_scatter(send, 'inter', scatter_dimension=0, tiled=True)  71.8 us
    all_to_all x1, blocking collectives, on_device(): lax.all_to_all(summed.reshape(intra_size, TILE, width), 'intra', 0, 0, ti...  24.3 us
    all_to_all x1, blocking collectives, on_device(): lax.all_to_all(placed.reshape(intra_size, TILE, width), 'intra', 0, 0, ti...  21.4 us
    pallas_call x2, Pallas kernels, over_planes(): pl.pallas_call(kernel, grid_spec=pltpu.PrefetchScalarGridSpec(num_scalar_...  18.6 us
  transfers between devices with their start and end apart: 2, of which 2 were waited for; matrix products, arithmetic and copies ran while one was open for 0% of the time, Pallas kernels for 4%

profile of v3, /device:TPU:1, one launch (start us, length us, event | category | flops | bytes accessed | tf_op | source)
XLA Modules:
  0.0 236.9 jit_solution(6374339080309448107)
XLA Ops:
  7.2 0.0 all-gather.2.cloned.1.call-start
  7.2 2.3 place.1
  9.5 21.4 %all_to_all.10 = bf16[32,8,768]{2,1,0:T(8,128)(2,1)} all-to-all(bf16[32,8,768]{2,1,0:T(8,128)(2,1)} %bitcast.20), channel_id=1, replica_groups=mesh['inter'=16,'intra'=32] {'intra'}, dimensions={0} | all-to-all | bytes 786432 | tf_op jit(solution)/shard_map/all_to_all | solution.py:152
  30.9 0.0 all-gather.2.cloned.1.call-update
  30.9 0.0 reduce-scatter.2.cloned.1.call-start
  31.0 82.2 %all-gather.2.cloned.1.call-done.rows = bf16[16,256,768]{2,1,0:T(8,128)(2,1)} async-done(((bf16[1,256,768]{2,1,0:T(8,128)(2,1)}), bf16[16,256,768]{2,1,0:T(8,128)(2,1)}) %all-gather.2.cloned.1.call-update) | async-done | bytes 6291472 | tf_op jit(solution)/shard_map/all_gather | solution.py:153
  113.2 10.0 %expert.1 = bf16[16,256,768]{2,1,0:T(8,128)(2,1)} custom-call(s32[1]{0:T(128)} %bitcast.group_ref, bf16[16,256,768]{2,1,0:T(8,128)(2,1)} %all-gather.2.cloned.1.call-done.rows, bf16[768,384]{1,0:T(8,128)(2,1)} %bitcast.14, bf16[384,768]{1,0:T(8,128)(2,1)} %bitcast.16), custom_call_target="tpu_custom_call" | custom-call | tf_op jit(solution)/shard_map/expert/pallas_call | solution.py:164
  123.2 0.0 reduce-scatter.2.cloned.1.call-update
  123.2 8.6 %weight_grads.1 = (bf16[768,384]{1,0:T(8,128)(2,1)}, bf16[384,768]{1,0:T(8,128)(2,1)}) custom-call(s32[1]{0:T(128)} %bitcast.group_ref, bf16[16,256,768]{2,1,0:T(8,128)(2,1)} %all-gather.2.cloned.1.call-done.rows, bf16[768,384]{1,0:T(8,128)(2,1)} %bitcast.15, bf16[384,768]{1,0:T(8,128)(2,1)} %bitcast.17), custom_call_target="tpu_custom_call" | custom-call | tf_op jit(solution)/shard_map/weight_grads/pallas_call | solution.py:164
  131.8 71.8 %reduce-scatter.2.cloned.1.call-done = bf16[1,256,768]{2,1,0:T(8,128)(2,1)} async-done(((bf16[16,256,768]{2,1,0:T(8,128)(2,1)}), bf16[1,256,768]{2,1,0:T(8,128)(2,1)}) %reduce-scatter.2.cloned.1.call-update) | async-done | bytes 393232 | tf_op jit(solution)/shard_map/reduce_scatter | solution.py:181
  203.5 24.3 %all_to_all.11 = bf16[32,8,768]{2,1,0:T(8,128)(2,1)} all-to-all(bf16[32,8,768]{2,1,0:T(8,128)(2,1)} %bitcast.21), channel_id=1, replica_groups=mesh['inter'=16,'intra'=32] {'intra'}, dimensions={0} | all-to-all | bytes 786432 | tf_op jit(solution)/shard_map/all_to_all | solution.py:191
  227.8 2.2 pick.1
Async XLA Ops:
  7.2 106.0 %all-gather.2.cloned.1.call-start = ((), (), s32[]{:S(2)}) async-start(), calls=%async_computation.3 | async-start | bytes 6684672 | tf_op jit(solution)/shard_map/all_gather | solution.py:153
  30.9 172.6 %reduce-scatter.2.cloned.1.call-start = ((), (), s32[]{:S(2)}) async-start(), calls=%async_computation.4 | async-start | bytes 6684672 | tf_op jit(solution)/shard_map/reduce_scatter | solution.py:181
Sparse Core Ops, SparseCore 0:
  31.0 82.1 all-gather.1
  123.3 80.1 reduce-scatter.1

commit v4 on v3

--- a/solution.py
+++ b/solution.py
@@ -75,54 +75,54 @@
     token_grad[...] = dot((at == row + CAP).astype(jnp.bfloat16), home[...]).astype(jnp.bfloat16)
 
 
-def row_places(narrow, wide, first, transposed):
-    half = narrow // KINDS
-    shape = (wide, narrow) if transposed else (narrow, wide)
+def row_order(wide, transposed):
+    half = wide // TILE * CAP
+    shape = (wide, wide)
     index = lax.broadcasted_iota(jnp.int32, shape, 1 if transposed else 0)
     at = lax.broadcasted_iota(jnp.int32, shape, 0 if transposed else 1)
-    kind = (index >= half).astype(jnp.int32)
-    within = index - kind * half
-    return (at == (within >> 1) * TILE + first + kind * CAP + (within & 1)).astype(jnp.bfloat16)
-
-
-def forward_rows(group_ref, rows, weight_in, weight_out, rows_x, rows_g):
-    sources, wide, _ = rows.shape
-    narrow = wide // EGRP
+    part = sum((index >= half * k).astype(jnp.int32) for k in range(1, EGRP * KINDS))
+    within = index - part * half
+    return (at == (within >> 1) * TILE + part * CAP + (within & 1)).astype(jnp.bfloat16)
+
+
+def order_kernel(transposed, rows, ordered):
+    ordered[...] = dot(row_order(rows.shape[0], transposed), rows[...]).astype(jnp.bfloat16)
+
+
+def forward_rows(rows, weight_in, weight_out):
+    sources, narrow, width = rows.shape
     half = narrow // KINDS
-    take = row_places(narrow, wide, group_ref[0] * (KINDS * CAP), False)
-    for s in range(sources):
-        taken = dot(take, rows[s]).astype(jnp.bfloat16)
-        rows_x[pl.ds(s * half, half), :] = taken[:half]
-        rows_g[pl.ds(s * half, half), :] = taken[half:]
-    pre_act = dot(rows_x[...], weight_in[...])
-    hidden_grad = dot(rows_g[...], weight_out[...], ((1,), (1,)))
+    rows_x = rows[:, :half, :].reshape(sources * half, width)
+    rows_g = rows[:, half:, :].reshape(sources * half, width)
+    pre_act = dot(rows_x, weight_in[...])
+    hidden_grad = dot(rows_g, weight_out[...], ((1,), (1,)))
     value, slope = gelu_and_slope(pre_act)
-    return value.astype(jnp.bfloat16), (hidden_grad * slope).astype(jnp.bfloat16)
-
-
-def expert_kernel(group_ref, rows, weight_in, weight_out, send, rows_x, rows_g):
-    sources, wide, _ = rows.shape
-    narrow = wide // EGRP
+    return rows_x, rows_g, value.astype(jnp.bfloat16), (hidden_grad * slope).astype(jnp.bfloat16)
+
+
+def expert_kernel(group_ref, rows, weight_in, weight_out, send):
+    sources, narrow, width = rows.shape
     half = narrow // KINDS
-    hidden, pre_grad = forward_rows(group_ref, rows, weight_in, weight_out, rows_x, rows_g)
+    _, _, hidden, pre_grad = forward_rows(rows, weight_in, weight_out)
     part_out = dot(hidden, weight_out[...]).astype(jnp.bfloat16)
     part_in = dot(pre_grad, weight_in[...], ((1,), (1,))).astype(jnp.bfloat16)
-    put = row_places(narrow, wide, group_ref[0] * (KINDS * CAP), True)
-    for s in range(sources):
-        both = jnp.concatenate([part_out[s * half : (s + 1) * half], part_in[s * half : (s + 1) * half]], axis=0)
-        send[s] = dot(put, both).astype(jnp.bfloat16)
-
-
-def weights_kernel(group_ref, rows, weight_in, weight_out, grad_in, grad_out, rows_x, rows_g, sum_in, sum_out):
-    hidden, pre_grad = forward_rows(group_ref, rows, weight_in, weight_out, rows_x, rows_g)
+    own = pl.multiple_of(group_ref[0] * narrow, narrow)
+    other = pl.multiple_of((EGRP - 1 - group_ref[0]) * narrow, narrow)
+    send[:, pl.ds(other, narrow), :] = jnp.zeros((sources, narrow, width), jnp.bfloat16)
+    send[:, pl.ds(own, half), :] = part_out.reshape(sources, half, width)
+    send[:, pl.ds(own + half, half), :] = part_in.reshape(sources, half, width)
+
+
+def weights_kernel(group_ref, rows, weight_in, weight_out, grad_in, grad_out, sum_in, sum_out):
+    rows_x, rows_g, hidden, pre_grad = forward_rows(rows, weight_in, weight_out)
 
     @pl.when(pl.program_id(0) == 0)
     def _():
         sum_in[...] = jnp.zeros_like(sum_in)
         sum_out[...] = jnp.zeros_like(sum_out)
 
-    sum_in[...] += dot(rows_x[...], pre_grad, ((0,), (0,)))
-    sum_out[...] += dot(hidden, rows_g[...], ((0,), (0,)))
+    sum_in[...] += dot(rows_x, pre_grad, ((0,), (0,)))
+    sum_out[...] += dot(hidden, rows_g, ((0,), (0,)))
 
     @pl.when(pl.program_id(0) == pl.num_programs(0) - 1)
     def _():
@@ -150,15 +150,25 @@
         name="place",
     )(tokens, *routing, out_grad)
     moved = lax.all_to_all(placed.reshape(intra_size, TILE, width), "intra", 0, 0, tiled=True)
-    spread = lax.all_gather(moved.reshape(1, wide, width), "inter", axis=0, tiled=True)
+
+    def reorder(rows, transposed, name):
+        return pl.pallas_call(
+            functools.partial(order_kernel, transposed),
+            out_shape=jax.ShapeDtypeStruct((wide, width), jnp.bfloat16),
+            compiler_params=params,
+            name=name,
+        )(rows.reshape(wide, width))
+
+    ordered = reorder(moved, False, "order")
+    spread = lax.all_gather(ordered[None], "inter", axis=0, tiled=True)
 
     step = 4
-    rows_step = step * wide // (EGRP * KINDS)
+    narrow = wide // EGRP
     whole = lambda i, *_: (0, 0)
     by_plane = pl.BlockSpec((step, wide, width), lambda i, *_: (i, 0, 0))
     in_block = pl.BlockSpec((width, hidden_units), whole)
     out_block = pl.BlockSpec((hidden_units, width), whole)
-    row_scratch = [pltpu.VMEM((rows_step, width), jnp.bfloat16)] * 2
+    own_rows = pl.BlockSpec((step, narrow, width), lambda i, group_ref: (i, group_ref[0], 0))
 
     def over_planes(kernel, name, out_specs, out_shape, scratch):
         return pl.pallas_call(
@@ -166,9 +176,9 @@
             grid_spec=pltpu.PrefetchScalarGridSpec(
                 num_scalar_prefetch=1,
                 grid=(inter_size // step,),
-                in_specs=[by_plane, in_block, out_block],
+                in_specs=[own_rows, in_block, out_block],
                 out_specs=out_specs,
-                scratch_shapes=row_scratch + scratch,
+                scratch_shapes=scratch,
             ),
             out_shape=out_shape,
             compiler_params=params,
@@ -188,7 +198,8 @@
     )
     summed, out_weight_grad, in_weight_grad = lax.optimization_barrier((summed, out_weight_grad, in_weight_grad))
 
-    home = lax.all_to_all(summed.reshape(intra_size, TILE, width), "intra", 0, 0, tiled=True)
+    back = reorder(summed, True, "restore")
+    home = lax.all_to_all(back.reshape(intra_size, TILE, width), "intra", 0, 0, tiled=True)
     expert_out, gate_grad, token_grad = pl.pallas_call(
         functools.partial(pick_kernel, intra_size),
         out_shape=[
@@ -196,7 +207,7 @@
             jax.ShapeDtypeStruct((1, tok_rows), jnp.float32),
             jax.ShapeDtypeStruct((tok_rows, width), jnp.bfloat16),
         ],
-        compiler_params=params,
+        compiler_params=pltpu.CompilerParams(vmem_limit_bytes=16 * 1024 * 1024),
         name="pick",
     )(home.reshape(wide, width), *routing, out_grad)
     return (

time: 237 us -> 238 us (level)
    pallas_call x0 -> x2, Pallas kernels: none -> 4.02 us  [reorder(): pl.pallas_call(functools.partial(order_kernel, transposed), out_shape=jax...]
    pallas_call x2, Pallas kernels: 18.6 us -> 15.2 us  [over_planes(): pl.pallas_call(kernel, grid_spec=pltpu.PrefetchScalarGridSpec(num_scalar_...]
  transfers between devices with their start and end apart: 2 -> 2, of which waited for: 2 -> 2; matrix products, arithmetic and copies ran while one was open for 0% -> 0% of each run, Pallas kernels for 4% -> 3%
where the time goes in v4:
time: 238 us; the launch traced here: 237 us
  waiting for transfers between devices  155 us (65%)
  blocking collectives  45.9 us (19%)
  Pallas kernels  22.6 us (9%)
  between operations  14.1 us (6%)
    all_gather x1, waiting for transfers between devices, on_device(): spread = lax.all_gather(ordered[None], 'inter', axis=0, tiled=True)  82.2 us
    reduce_scatter x1, waiting for transfers between devices, on_device(): summed = lax.psum_scatter(send, 'inter', scatter_dimension=0, tiled=True)  72.3 us
    all_to_all x1, blocking collectives, on_device(): lax.all_to_all(back.reshape(intra_size, TILE, width), 'intra', 0, 0, tile...  24.5 us
    all_to_all x1, blocking collectives, on_device(): lax.all_to_all(placed.reshape(intra_size, TILE, width), 'intra', 0, 0, ti...  21.4 us
    pallas_call x2, Pallas kernels, over_planes(): pl.pallas_call(kernel, grid_spec=pltpu.PrefetchScalarGridSpec(num_scalar_...  15.2 us
  transfers between devices with their start and end apart: 2, of which 2 were waited for; matrix products, arithmetic and copies ran while one was open for 0% of the time, Pallas kernels for 3%

profile of v4, /device:TPU:1, one launch (start us, length us, event | category | flops | bytes accessed | tf_op | source)
XLA Modules:
  0.0 237.3 jit_solution(942624842643143831)
XLA Ops:
  7.2 0.0 all-gather.3.cloned.1.call-start
  7.2 2.3 place.1
  9.5 21.4 %all_to_all.10 = bf16[32,8,768]{2,1,0:T(8,128)(2,1)} all-to-all(bf16[32,8,768]{2,1,0:T(8,128)(2,1)} %bitcast.33), channel_id=1, replica_groups=mesh['inter'=16,'intra'=32] {'intra'}, dimensions={0} | all-to-all | bytes 786432 | tf_op jit(solution)/shard_map/all_to_all | solution.py:152
  30.9 2.0 order.1
  32.9 0.0 all-gather.3.cloned.1.call-update
  32.9 0.0 reduce-scatter.2.cloned.1.call-start
  33.0 82.2 %all-gather.3.cloned.1.call-done = bf16[4096,768]{1,0:T(8,128)(2,1)} async-done(((bf16[256,768]{1,0:T(8,128)(2,1)}), bf16[4096,768]{1,0:T(8,128)(2,1)}) %all-gather.3.cloned.1.call-update) | async-done | bytes 6291472 | tf_op jit(solution)/shard_map/all_gather | solution.py:163
  115.2 7.4 %expert.1 = bf16[16,256,768]{2,1,0:T(8,128)(2,1)} custom-call(s32[1]{0:T(128)} %bitcast.group_ref, bf16[16,256,768]{2,1,0:T(8,128)(2,1)} %bitcast.25, bf16[768,384]{1,0:T(8,128)(2,1)} %bitcast.27, bf16[384,768]{1,0:T(8,128)(2,1)} %bitcast.29), custom_call_target="tpu_custom_call" | custom-call | tf_op jit(solution)/shard_map/expert/pallas_call | solution.py:174
  122.6 0.0 copy-start
  122.6 0.0 copy-start.1
  122.6 0.0 copy-start.2
  122.6 0.0 copy-start.3
  122.6 0.0 copy-start.4
  122.6 0.0 reduce-scatter.2.cloned.1.call-update
  122.6 7.8 %weight_grads.1 = (bf16[768,384]{1,0:T(8,128)(2,1)}, bf16[384,768]{1,0:T(8,128)(2,1)}) custom-call(s32[1]{0:T(128)} %bitcast.group_ref, bf16[16,256,768]{2,1,0:T(8,128)(2,1)} %bitcast.26, bf16[768,384]{1,0:T(8,128)(2,1)} %bitcast.28, bf16[384,768]{1,0:T(8,128)(2,1)} %bitcast.30), custom_call_target="tpu_custom_call" | custom-call | tf_op jit(solution)/shard_map/weight_grads/pallas_call | solution.py:174
  130.5 72.3 %reduce-scatter.2.cloned.1.call-done = bf16[1,256,768]{2,1,0:T(8,128)(2,1)} async-done(((bf16[16,256,768]{2,1,0:T(8,128)(2,1)}), bf16[1,256,768]{2,1,0:T(8,128)(2,1)}) %reduce-scatter.2.cloned.1.call-update) | async-done | bytes 393232 | tf_op jit(solution)/shard_map/reduce_scatter | solution.py:191
  202.7 2.0 restore.1
  204.8 24.5 %all_to_all.11 = bf16[32,8,768]{2,1,0:T(8,128)(2,1)S(1)} all-to-all(bf16[32,8,768]{2,1,0:T(8,128)(2,1)} %bitcast.32), channel_id=1, replica_groups=mesh['inter'=16,'intra'=32] {'intra'}, dimensions={0} | all-to-all | bytes 786432 | tf_op jit(solution)/shard_map/all_to_all | solution.py:202
  229.3 0.0 copy-done
  229.3 0.0 copy-done.1
  229.3 0.0 copy-done.2
  229.3 0.0 copy-done.3
  229.3 0.0 copy-done.4
  229.3 1.1 pick.1
Async XLA Ops:
  7.2 108.0 %all-gather.3.cloned.1.call-start = ((), (), s32[]{:S(2)}) async-start(), calls=%async_computation.4 | async-start | bytes 6684672 | tf_op jit(solution)/shard_map/all_gather | solution.py:163
  32.9 169.8 %reduce-scatter.2.cloned.1.call-start = ((), (), s32[]{:S(2)}) async-start(), calls=%async_computation.3 | async-start | bytes 6684672 | tf_op jit(solution)/shard_map/reduce_scatter | solution.py:191
  122.6 106.7 %copy-start = (bf16[128,768]{1,0:T(8,128)(2,1)S(1)}, bf16[128,768]{1,0:T(8,128)(2,1)}, u32[]{:S(2)}) copy-start(bf16[128,768]{1,0:T(8,128)(2,1)} %out_grad.3) | copy-start | bytes 589828
  122.6 106.7 %copy-start.1 = (s32[128]{0:T(128)S(1)}, s32[128]{0:T(128)}, u32[]{:S(2)}) copy-start(s32[128]{0:T(128)} %param.9) | copy-start | bytes 1540
  122.6 106.7 %copy-start.2 = (s32[128]{0:T(128)S(1)}, s32[128]{0:T(128)}, u32[]{:S(2)}) copy-start(s32[128]{0:T(128)} %param.10) | copy-start | bytes 1540
  122.6 106.7 %copy-start.3 = (s32[128]{0:T(128)S(1)}, s32[128]{0:T(128)}, u32[]{:S(2)}) copy-start(s32[128]{0:T(128)} %param.11) | copy-start | bytes 1540
  122.6 106.7 %copy-start.4 = (f32[128]{0:T(128)S(1)}, f32[128]{0:T(128)}, u32[]{:S(2)}) copy-start(f32[128]{0:T(128)} %param.12) | copy-start | bytes 1540
Sparse Core Ops, SparseCore 0:
  33.0 82.1 all-gather.2
  122.8 79.9 reduce-scatter.1

commit v5 on v4

--- a/solution.py
+++ b/solution.py
@@ -13,6 +13,8 @@
 KINDS = 2
 TILE = EGRP * KINDS * CAP
 VMEM_BYTES = 60 * 1024 * 1024
+VMEM_SMALL = 8 * 1024 * 1024
+SMALLEST = 2.0**-126
 
 gelu_root = math.sqrt(2.0 / math.pi)
 gelu_cubic = 0.044715
@@ -85,15 +87,33 @@
     return (at == (within >> 1) * TILE + part * CAP + (within & 1)).astype(jnp.bfloat16)
 
 
+def encode(value):
+    size = jnp.maximum(jnp.abs(value), SMALLEST)
+    exponent = jnp.floor(jnp.log2(size))
+    code = jnp.round((exponent + 126.0) * 128.0 + size * jnp.exp2(-exponent) * 128.0)
+    code = jnp.where(jnp.abs(value) < SMALLEST, 0.0, code)
+    return jnp.where(value < 0.0, -code, code).astype(jnp.int32).astype(jnp.int16)
+
+
+def decode(code):
+    wide = code.astype(jnp.int32)
+    size = jnp.abs(wide)
+    mantissa = ((size & 127) + 128).astype(jnp.float32) * (1.0 / 128.0)
+    value = mantissa * jnp.exp2((size >> 7).astype(jnp.float32) - 127.0)
+    value = jnp.where(size < 128, 0.0, value)
+    return jnp.where(wide < 0, -value, value).astype(jnp.bfloat16)
+
+
 def order_kernel(transposed, rows, ordered):
-    ordered[...] = dot(row_order(rows.shape[0], transposed), rows[...]).astype(jnp.bfloat16)
+    moved = dot(row_order(rows.shape[0], transposed), rows[...])
+    ordered[...] = moved.astype(jnp.bfloat16) if transposed else encode(moved)
 
 
 def forward_rows(rows, weight_in, weight_out):
     sources, narrow, width = rows.shape
     half = narrow // KINDS
-    rows_x = rows[:, :half, :].reshape(sources * half, width)
-    rows_g = rows[:, half:, :].reshape(sources * half, width)
+    rows_x = decode(rows[:, :half, :]).reshape(sources * half, width)
+    rows_g = decode(rows[:, half:, :]).reshape(sources * half, width)
     pre_act = dot(rows_x, weight_in[...])
     hidden_grad = dot(rows_g, weight_out[...], ((1,), (1,)))
     value, slope = gelu_and_slope(pre_act)
@@ -154,8 +174,8 @@
     def reorder(rows, transposed, name):
         return pl.pallas_call(
             functools.partial(order_kernel, transposed),
-            out_shape=jax.ShapeDtypeStruct((wide, width), jnp.bfloat16),
-            compiler_params=params,
+            out_shape=jax.ShapeDtypeStruct((wide, width), jnp.bfloat16 if transposed else jnp.int16),
+            compiler_params=pltpu.CompilerParams(vmem_limit_bytes=VMEM_SMALL),
             name=name,
         )(rows.reshape(wide, width))
 
@@ -207,7 +227,7 @@
             jax.ShapeDtypeStruct((1, tok_rows), jnp.float32),
             jax.ShapeDtypeStruct((tok_rows, width), jnp.bfloat16),
         ],
-        compiler_params=pltpu.CompilerParams(vmem_limit_bytes=16 * 1024 * 1024),
+        compiler_params=pltpu.CompilerParams(vmem_limit_bytes=VMEM_SMALL),
         name="pick",
     )(home.reshape(wide, width), *routing, out_grad)
     return (

time: 238 us -> 235 us (0.987)
  waiting for transfers between devices: 155 us -> 81.6 us
  blocking collectives: 45.9 us -> 104 us
  starting transfers between devices: 0.08 us -> 10.5 us
    all_gather x1 -> x0, waiting for transfers between devices: 82.2 us -> none  [on_device(): spread = lax.all_gather(ordered[None], 'inter', axis=0, tiled=True)]
    all_gather x0 -> x1, blocking collectives: none -> 79.2 us  [on_device(): spread = lax.all_gather(ordered[None], 'inter', axis=0, tiled=True)]
    all_to_all x1 -> x0, blocking collectives: 21.4 us -> none  [on_device(): lax.all_to_all(placed.reshape(intra_size, TILE, width), 'intra', 0, 0, ti...]
    all_to_all x0 -> x1, starting transfers between devices: none -> 10.4 us  [on_device(): lax.all_to_all(placed.reshape(intra_size, TILE, width), 'intra', 0, 0, ti...]
    all_to_all x0 -> x1, waiting for transfers between devices: none -> 10.2 us  [on_device(): lax.all_to_all(placed.reshape(intra_size, TILE, width), 'intra', 0, 0, ti...]
    pallas_call x2, Pallas kernels: 15.2 us -> 19.3 us  [over_planes(): pl.pallas_call(kernel, grid_spec=pltpu.PrefetchScalarGridSpec(num_scalar_...]
    pallas_call x2, Pallas kernels: 4.02 us -> 0.95 us  [reorder(): pl.pallas_call(functools.partial(order_kernel, transposed), out_shape=jax...]
  transfers between devices with their start and end apart: 2 -> 2, of which waited for: 2 -> 2; matrix products, arithmetic and copies ran while one was open for 0% -> 0% of each run, Pallas kernels for 3% -> 4%
where the time goes in v5:
time: 235 us
  blocking collectives  104 us (44%)
  waiting for transfers between devices  81.6 us (35%)
  Pallas kernels  23.7 us (10%)
  between operations  14.1 us (6%)
  starting transfers between devices  10.5 us (4%)
    all_gather x1, blocking collectives, on_device(): spread = lax.all_gather(ordered[None], 'inter', axis=0, tiled=True)  79.2 us
    reduce_scatter x1, waiting for transfers between devices, on_device(): summed = lax.psum_scatter(send, 'inter', scatter_dimension=0, tiled=True)  71.4 us
    all_to_all x1, blocking collectives, on_device(): lax.all_to_all(back.reshape(intra_size, TILE, width), 'intra', 0, 0, tile...  24.6 us
    pallas_call x2, Pallas kernels, over_planes(): pl.pallas_call(kernel, grid_spec=pltpu.PrefetchScalarGridSpec(num_scalar_...  19.3 us
    all_to_all x1, starting transfers between devices, on_device(): lax.all_to_all(placed.reshape(intra_size, TILE, width), 'intra', 0, 0, ti...  10.4 us
    all_to_all x1, waiting for transfers between devices, on_device(): lax.all_to_all(placed.reshape(intra_size, TILE, width), 'intra', 0, 0, ti...  10.2 us
  transfers between devices with their start and end apart: 2, of which 2 were waited for; matrix products, arithmetic and copies ran while one was open for 0% of the time, Pallas kernels for 4%

profile of v5, /device:TPU:1, one launch (start us, length us, event | category | flops | bytes accessed | tf_op | source)
XLA Modules:
  0.0 234.7 jit_solution(1969048404882755136)
XLA Ops:
  7.2 2.3 place.1
  9.4 10.4 %all-to-all-start = ((bf16[32,8,768]{2,1,0:T(8,128)(2,1)}), bf16[32,8,768]{2,1,0:T(8,128)(2,1)S(1)}, u32[]{:S(2)}, u32[]{:S(2)}) async-start(bf16[32,8,768]{2,1,0:T(8,128)(2,1)} %bitcast.34), calls=%async_computation | async-start | bytes 786432 | tf_op jit(solution)/shard_map/all_to_all | solution.py:172
  19.9 0.0 reduce-scatter.2.cloned.1.call-start
  19.9 10.2 %all-to-all-done = bf16[32,8,768]{2,1,0:T(8,128)(2,1)S(1)} async-done(((bf16[32,8,768]{2,1,0:T(8,128)(2,1)}), bf16[32,8,768]{2,1,0:T(8,128)(2,1)S(1)}, u32[]{:S(2)}, u32[]{:S(2)}) %all-to-all-start) | async-done | bytes 393248 | tf_op jit(solution)/shard_map/all_to_all | solution.py:172
  30.1 0.7 order.1
  30.8 79.2 %all-gather.2 = s16[4096,768]{1,0:T(8,128)(2,1)} all-gather(s16[256,768]{1,0:T(8,128)(2,1)S(1)} %order.1), channel_id=2, replica_groups=mesh['inter'=16,'intra'=32] {'inter'}, dimensions={0}, use_global_device_ids=true | all-gather | bytes 6684672 | tf_op jit(solution)/shard_map/all_gather | solution.py:183
  110.1 9.2 %expert.1 = bf16[16,256,768]{2,1,0:T(8,128)(2,1)} custom-call(s32[1]{0:T(128)} %bitcast.group_ref, s16[16,256,768]{2,1,0:T(8,128)(2,1)} %bitcast.28, bf16[768,384]{1,0:T(8,128)(2,1)} %bitcast.30, bf16[384,768]{1,0:T(8,128)(2,1)} %bitcast.32), custom_call_target="tpu_custom_call" | custom-call | tf_op jit(solution)/shard_map/expert/pallas_call | solution.py:194
  119.3 0.0 copy-start
  119.3 0.0 copy-start.2
  119.3 0.0 copy-start.3
  119.3 0.0 copy-start.4
  119.3 0.0 copy-start.5
  119.3 0.0 reduce-scatter.2.cloned.1.call-update
  119.3 10.1 %weight_grads.1 = (bf16[768,384]{1,0:T(8,128)(2,1)}, bf16[384,768]{1,0:T(8,128)(2,1)}) custom-call(s32[1]{0:T(128)} %bitcast.group_ref, s16[16,256,768]{2,1,0:T(8,128)(2,1)} %bitcast.29, bf16[768,384]{1,0:T(8,128)(2,1)} %bitcast.31, bf16[384,768]{1,0:T(8,128)(2,1)} %bitcast.33), custom_call_target="tpu_custom_call" | custom-call | tf_op jit(solution)/shard_map/weight_grads/pallas_call | solution.py:194
  129.5 71.4 %reduce-scatter.2.cloned.1.call-done = bf16[1,256,768]{2,1,0:T(8,128)(2,1)} async-done(((bf16[16,256,768]{2,1,0:T(8,128)(2,1)}), bf16[1,256,768]{2,1,0:T(8,128)(2,1)}) %reduce-scatter.2.cloned.1.call-update) | async-done | bytes 393232 | tf_op jit(solution)/shard_map/reduce_scatter | solution.py:211
  200.8 0.0 copy-start.1
  200.8 1.0 copy-done.1
  201.8 0.3 restore.1
  202.1 24.6 %all_to_all.10 = bf16[32,8,768]{2,1,0:T(8,128)(2,1)S(1)} all-to-all(bf16[32,8,768]{2,1,0:T(8,128)(2,1)S(1)} %bitcast.18), channel_id=1, replica_groups=mesh['inter'=16,'intra'=32] {'intra'}, dimensions={0} | all-to-all | bytes 786432 | tf_op jit(solution)/shard_map/all_to_all | solution.py:222
  226.7 0.0 copy-done
  226.7 0.0 copy-done.2
  226.7 0.0 copy-done.3
  226.8 0.0 copy-done.4
  226.8 0.0 copy-done.5
  226.8 1.1 pick.1
Async XLA Ops:
  9.4 20.7 %all-to-all-start = ((bf16[32,8,768]{2,1,0:T(8,128)(2,1)}), bf16[32,8,768]{2,1,0:T(8,128)(2,1)S(1)}, u32[]{:S(2)}, u32[]{:S(2)}) async-start(bf16[32,8,768]{2,1,0:T(8,128)(2,1)} %bitcast.34), calls=%async_computation | async-start | bytes 786432 | tf_op jit(solution)/shard_map/all_to_all | solution.py:172
  19.9 181.0 %reduce-scatter.2.cloned.1.call-start = ((), (), s32[]{:S(2)}) async-start(), calls=%async_computation.3 | async-start | bytes 6684672 | tf_op jit(solution)/shard_map/reduce_scatter | solution.py:211
  119.3 107.5 %copy-start = (bf16[128,768]{1,0:T(8,128)(2,1)S(1)}, bf16[128,768]{1,0:T(8,128)(2,1)}, u32[]{:S(2)}) copy-start(bf16[128,768]{1,0:T(8,128)(2,1)} %out_grad.3) | copy-start | bytes 589828
  119.3 107.5 %copy-start.2 = (s32[128]{0:T(128)S(1)}, s32[128]{0:T(128)}, u32[]{:S(2)}) copy-start(s32[128]{0:T(128)} %param.9) | copy-start | bytes 1540
  119.3 107.5 %copy-start.3 = (s32[128]{0:T(128)S(1)}, s32[128]{0:T(128)}, u32[]{:S(2)}) copy-start(s32[128]{0:T(128)} %param.10) | copy-start | bytes 1540
  119.3 107.5 %copy-start.4 = (s32[128]{0:T(128)S(1)}, s32[128]{0:T(128)}, u32[]{:S(2)}) copy-start(s32[128]{0:T(128)} %param.11) | copy-start | bytes 1540
  119.3 107.5 %copy-start.5 = (f32[128]{0:T(128)S(1)}, f32[128]{0:T(128)}, u32[]{:S(2)}) copy-start(f32[128]{0:T(128)} %param.12) | copy-start | bytes 1540
  200.8 1.0 copy-start.1
Sparse Core Ops, SparseCore 0:
  119.5 81.3 reduce-scatter.1

commit v6 on v4

v6 whole, which is shorter than its diff:
```python
import functools
import math

import jax
import jax.numpy as jnp
from jax import lax
from jax.experimental import pallas as pl
from jax.experimental.pallas import tpu as pltpu
from jax.sharding import PartitionSpec as P

EGRP = 2
CAP = 2
KINDS = 2
TILE = KINDS * CAP
VMEM_BYTES = 60 * 1024 * 1024
VMEM_SMALL = 8 * 1024 * 1024
STEPS = 229.0
OCTAVES = 140.0
SMALLEST = 2.0**-126

gelu_root = math.sqrt(2.0 / math.pi)
gelu_cubic = 0.044715


def gelu_and_slope(pre_value):
    square = pre_value * pre_value
    argument = gelu_root * (pre_value + gelu_cubic * square * pre_value)
    slope_tanh = jnp.tanh(argument)
    half_up = 0.5 * (1.0 + slope_tanh)
    value = pre_value * half_up
    slope = half_up + 0.5 * pre_value * (1.0 - slope_tanh * slope_tanh) * gelu_root * (
        1.0 + 3.0 * gelu_cubic * square
    )
    return value, slope


def dot(left, right, dims=((1,), (0,))):
    return lax.dot_general(left, right, (dims, ((), ())), preferred_element_type=jnp.float32)


def encode(value):
    size = jnp.abs(value)
    code = jnp.round((jnp.log2(jnp.maximum(size, SMALLEST)) + OCTAVES) * STEPS)
    code = jnp.where(size < SMALLEST, 0.0, code)
    return jnp.where(value < 0.0, -code, code).astype(jnp.int32).astype(jnp.int16)


def decode(code):
    wide = code.astype(jnp.int32).astype(jnp.float32)
    value = jnp.exp2(jnp.abs(wide) * (1.0 / STEPS) - OCTAVES)
    return jnp.where(wide < 0.0, -value, value).astype(jnp.bfloat16)


def as_column(row):
    count = row.shape[1]
    shape = (count, count)
    diagonal = lax.broadcasted_iota(jnp.int32, shape, 0) == lax.broadcasted_iota(jnp.int32, shape, 1)
    return jnp.sum(jnp.where(diagonal, row, 0.0), axis=1, keepdims=True)


def as_row(column):
    count = column.shape[0]
    shape = (count, count)
    diagonal = lax.broadcasted_iota(jnp.int32, shape, 0) == lax.broadcasted_iota(jnp.int32, shape, 1)
    return jnp.sum(jnp.where(diagonal, column, 0.0), axis=0, keepdims=True)


def slot_row(experts, slots, keep):
    return jnp.where(keep == 1, experts * TILE + slots, -TILE)


def place_kernel(tokens, experts, slots, keep, gate, out_grad, send):
    count = tokens.shape[0]
    row = slot_row(experts[...], slots[...], keep[...])
    scaled = (as_column(gate[...]) * out_grad[...].astype(jnp.float32)).astype(jnp.bfloat16)
    at = lax.broadcasted_iota(jnp.int32, (send.shape[0], count), 0)
    hot_x = (at == row).astype(jnp.bfloat16)
    hot_g = (at == row + CAP).astype(jnp.bfloat16)
    send[...] = (dot(hot_x, tokens[...]) + dot(hot_g, scaled)).astype(jnp.bfloat16)


def pick_kernel(home, experts, slots, keep, gate, out_grad, expert_out, gate_grad, token_grad):
    count = out_grad.shape[0]
    row = slot_row(experts[...], slots[...], keep[...])
    row = as_column(row.astype(jnp.float32)).astype(jnp.int32)
    at = lax.broadcasted_iota(jnp.int32, (count, home.shape[0]), 1)
    ffn_tok = dot((at == row).astype(jnp.bfloat16), home[...])
    expert_out[...] = (as_column(gate[...]) * ffn_tok).astype(jnp.bfloat16)
    gate_grad[...] = as_row(jnp.sum(out_grad[...].astype(jnp.float32) * ffn_tok, axis=1, keepdims=True))
    token_grad[...] = dot((at == row + CAP).astype(jnp.bfloat16), home[...]).astype(jnp.bfloat16)


def row_order(wide, transposed):
    half = wide // KINDS
    shape = (wide, wide)
    index = lax.broadcasted_iota(jnp.int32, shape, 1 if transposed else 0)
    at = lax.broadcasted_iota(jnp.int32, shape, 0 if transposed else 1)
    kind = (index >= half).astype(jnp.int32)
    within = index - half * kind
    return (at == (within >> 1) * TILE + kind * CAP + (within & 1)).astype(jnp.bfloat16)


def order_kernel(transposed, rows, ordered):
    moved = dot(row_order(rows.shape[0], transposed), rows[...])
    ordered[...] = moved.astype(jnp.bfloat16) if transposed else encode(moved)


def forward_rows(rows, weight_in, weight_out):
    sources, wide, width = rows.shape
    half = wide // KINDS
    rows_x = decode(rows[:, :half, :]).reshape(sources * half, width)
    rows_g = decode(rows[:, half:, :]).reshape(sources * half, width)
    pre_act = dot(rows_x, weight_in[...])
    hidden_grad = dot(rows_g, weight_out[...], ((1,), (1,)))
    value, slope = gelu_and_slope(pre_act)
    return rows_x, rows_g, value.astype(jnp.bfloat16), (hidden_grad * slope).astype(jnp.bfloat16)


def expert_kernel(rows, weight_in, weight_out, send):
    sources, wide, width = rows.shape
    half = wide // KINDS
    _, _, hidden, pre_grad = forward_rows(rows, weight_in, weight_out)
    part_out = dot(hidden, weight_out[...]).astype(jnp.bfloat16)
    part_in = dot(pre_grad, weight_in[...], ((1,), (1,))).astype(jnp.bfloat16)
    send[:, :half, :] = part_out.reshape(sources, half, width)
    send[:, half:, :] = part_in.reshape(sources, half, width)


def weights_kernel(rows, weight_in, weight_out, grad_in, grad_out, sum_in, sum_out):
    rows_x, rows_g, hidden, pre_grad = forward_rows(rows, weight_in, weight_out)

    @pl.when(pl.program_id(0) == 0)
    def _():
        sum_in[...] = jnp.zeros_like(sum_in)
        sum_out[...] = jnp.zeros_like(sum_out)

    sum_in[...] += dot(rows_x, pre_grad, ((0,), (0,)))
    sum_out[...] += dot(hidden, rows_g, ((0,), (0,)))

    @pl.when(pl.program_id(0) == pl.num_programs(0) - 1)
    def _():
        grad_in[...] = sum_in[...].astype(grad_in.dtype)
        grad_out[...] = sum_out[...].astype(grad_out.dtype)


def partner_groups(inter_size, intra_size):
    return [
        [plane * intra_size + index for plane in (low, inter_size - 1 - low) for index in range(intra_size)]
        for low in range(inter_size // EGRP)
    ]


def group_order(inter_size):
    blocks = inter_size // EGRP
    low = list(range(0, blocks, 2)) + list(range(blocks - 1 - blocks % 2, 0, -2))
    return [low, [inter_size - 1 - plane for plane in low]]


def on_device(tokens, expert_ids, slot_ids, keep_mask, gate_prob, out_grad, in_weight, out_weight):
    tok_rows, width = tokens.shape
    intra_size = lax.axis_size("intra")
    inter_size = lax.axis_size("inter")
    blocks_ff = inter_size // EGRP
    partners = EGRP * intra_size
    weight_in = in_weight[0, 0]
    weight_out = out_weight[0, 0]
    hidden_units = weight_in.shape[1]
    wide = partners * TILE
    params = pltpu.CompilerParams(vmem_limit_bytes=VMEM_BYTES)
    small = pltpu.CompilerParams(vmem_limit_bytes=VMEM_SMALL)
    routing = (expert_ids[None], slot_ids[None], keep_mask[None], gate_prob[None])
    groups = group_order(inter_size)

    def exchange(rows):
        moved = lax.all_to_all(
            rows.reshape(partners, TILE, width),
            ("inter", "intra"),
            0,
            0,
            axis_index_groups=partner_groups(inter_size, intra_size),
            tiled=True,
        )
        return moved.reshape(wide, width)

    def reorder(rows, transposed, name):
        return pl.pallas_call(
            functools.partial(order_kernel, transposed),
            out_shape=jax.ShapeDtypeStruct((wide, width), jnp.bfloat16 if transposed else jnp.int16),
            compiler_params=small,
            name=name,
        )(rows)

    placed = pl.pallas_call(
        place_kernel,
        out_shape=jax.ShapeDtypeStruct((wide, width), jnp.bfloat16),
        compiler_params=params,
        name="place",
    )(tokens, *routing, out_grad)
    ordered = reorder(exchange(placed), False, "order")
    spread = lax.all_gather(ordered, "inter", axis=0, axis_index_groups=groups, tiled=True)
    spread = spread.reshape(blocks_ff, wide, width)

    step = 2
    whole = lambda i: (0, 0)
    by_plane = pl.BlockSpec((step, wide, width), lambda i: (i, 0, 0))
    in_block = pl.BlockSpec((width, hidden_units), whole)
    out_block = pl.BlockSpec((hidden_units, width), whole)

    def over_planes(kernel, name, out_specs, out_shape, scratch):
        return pl.pallas_call(
            kernel,
            grid=(blocks_ff // step,),
            in_specs=[by_plane, in_block, out_block],
            out_specs=out_specs,
            scratch_shapes=scratch,
            out_shape=out_shape,
            compiler_params=params,
            name=name,
        )(spread, weight_in, weight_out)

    send = over_planes(
        expert_kernel, "expert", by_plane, jax.ShapeDtypeStruct((blocks_ff, wide, width), jnp.bfloat16), []
    )
    summed = lax.psum_scatter(
        send.reshape(blocks_ff * wide, width), "inter", scatter_dimension=0, axis_index_groups=groups, tiled=True
    )
    in_weight_grad, out_weight_grad = over_planes(
        weights_kernel,
        "weight_grads",
        [in_block, out_block],
        [jax.ShapeDtypeStruct(w.shape, jnp.bfloat16) for w in (weight_in, weight_out)],
        [pltpu.VMEM(w.shape, jnp.float32) for w in (weight_in, weight_out)],
    )
    summed, out_weight_grad, in_weight_grad = lax.optimization_barrier((summed, out_weight_grad, in_weight_grad))

    home = exchange(reorder(summed, True, "restore"))
    expert_out, gate_grad, token_grad = pl.pallas_call(
        pick_kernel,
        out_shape=[
            jax.ShapeDtypeStruct((tok_rows, width), jnp.bfloat16),
            jax.ShapeDtypeStruct((1, tok_rows), jnp.float32),
            jax.ShapeDtypeStruct((tok_rows, width), jnp.bfloat16),
        ],
        compiler_params=small,
        name="pick",
    )(home, *routing, out_grad)
    return (
        expert_out,
        gate_grad.reshape(tok_rows),
        token_grad,
        in_weight_grad[None, None],
        out_weight_grad[None, None],
    )


def solution(mesh):
    tok = P(("inter", "intra"), None)
    per = P(("inter", "intra"))
    wgt = P("inter", "intra", None, None)
    return jax.shard_map(
        on_device,
        mesh=mesh,
        in_specs=(tok, per, per, per, per, tok, wgt, wgt),
        out_specs=(tok, per, tok, wgt, wgt),
        check_vma=False,
    )
```

time: 238 us -> 240 us (level)
  blocking collectives: 45.9 us -> 140 us
  waiting for transfers between devices: 155 us -> 63.1 us
  Pallas kernels: 22.6 us -> 20.2 us
    all_gather x1 -> x0, waiting for transfers between devices: 82.2 us -> none  [on_device(): spread = lax.all_gather(ordered[None], 'inter', axis=0, tiled=True)]
    all_gather x0 -> x1, blocking collectives: none -> 62.3 us  [on_device(): lax.all_gather(ordered, 'inter', axis=0, axis_index_groups=groups, tiled=...]
    all_to_all x2, blocking collectives: 45.9 us -> 78 us  [exchange(): lax.all_to_all(rows.reshape(partners, TILE, width), ('inter', 'intra'), 0...]
    reduce_scatter x1, waiting for transfers between devices: 72.3 us -> 63.1 us  [on_device(): lax.psum_scatter(send.reshape(blocks_ff * wide, width), 'inter', scatter_...]
    pallas_call x2, Pallas kernels: 4.02 us -> 0.78 us  [reorder(): pl.pallas_call(functools.partial(order_kernel, transposed), out_shape=jax...]
  transfers between devices with their start and end apart: 2 -> 1, of which waited for: 2 -> 1; matrix products, arithmetic and copies ran while one was open for 0% -> 0% of each run, Pallas kernels for 3% -> 4%
where the time goes in v6:
time: 240 us
  blocking collectives  140 us (58%)
  waiting for transfers between devices  63.1 us (26%)
  Pallas kernels  20.2 us (8%)
  between operations  14.1 us (6%)
  local copies, waits for them, and re-layouts  2.4 us (1%)
    all_to_all x2, blocking collectives, exchange(): lax.all_to_all(rows.reshape(partners, TILE, width), ('inter', 'intra'), 0...  78 us
    reduce_scatter x1, waiting for transfers between devices, on_device(): lax.psum_scatter(send.reshape(blocks_ff * wide, width), 'inter', scatter_...  63.1 us
    all_gather x1, blocking collectives, on_device(): lax.all_gather(ordered, 'inter', axis=0, axis_index_groups=groups, tiled=...  62.3 us
    pallas_call x2, Pallas kernels, over_planes(): pl.pallas_call(kernel, grid=(blocks_ff // step,), in_specs=[by_plane, in_...  16 us
  transfers between devices with their start and end apart: 1, of which 1 were waited for; matrix products, arithmetic and copies ran while one was open for 0% of the time, Pallas kernels for 4%

profile of v6, /device:TPU:1, one launch (start us, length us, event | category | flops | bytes accessed | tf_op | source)
XLA Modules:
  0.0 240.1 jit_solution(2220242743689479700)
XLA Ops:
  7.2 0.0 reduce-scatter.2.cloned.1.call-start
  7.2 2.3 place.1
  9.5 1.1 reshape.31
  10.6 42.5 %all_to_all.10 = bf16[64,4,768]{2,1,0:T(4,128)(2,1)S(1)} all-to-all(bf16[64,4,768]{2,1,0:T(4,128)(2,1)S(1)} %reshape.31), channel_id=1, replica_groups={{0,1,2,3,4,5,6,7,8,9,10,11,12,13,14,15,16,17,18,19,20,21,22,23,24,25,26..., dimensions={0} | all-to-all | bytes 786432 | tf_op jit(solution)/shard_map/all_to_all | solution.py:175
  53.1 0.1 reshape.32.rows
  53.2 0.5 order.1
  53.7 62.3 %all-gather.1 = s16[2048,768]{1,0:T(8,128)(2,1)} all-gather(s16[256,768]{1,0:T(8,128)(2,1)S(1)} %order.1), channel_id=1, replica_groups={{0,64,128,192,224,160,96,32},{480,416,352,288,256,320,384,448},{1,65,12..., dimensions={0}, use_global_device_ids=true | all-gather | bytes 3538944 | tf_op jit(solution)/shard_map/all_gather | solution.py:200
  116.0 7.5 %expert.1 = bf16[8,256,768]{2,1,0:T(8,128)(2,1)} custom-call(s16[8,256,768]{2,1,0:T(8,128)(2,1)} %bitcast.19, bf16[768,384]{1,0:T(8,128)(2,1)} %bitcast.22, bf16[384,768]{1,0:T(8,128)(2,1)} %bitcast.24), custom_call_target="tpu_custom_call" | custom-call | tf_op jit(solution)/shard_map/expert/pallas_call | solution.py:210
  123.5 0.0 reduce-scatter.2.cloned.1.call-update
  123.5 0.0 copy-start
  123.5 0.0 copy-start.2
  123.6 0.0 copy-start.3
  123.6 0.0 copy-start.4
  123.6 0.0 copy-start.5
  123.6 8.5 %weight_grads.1 = (bf16[768,384]{1,0:T(8,128)(2,1)}, bf16[384,768]{1,0:T(8,128)(2,1)}) custom-call(s16[8,256,768]{2,1,0:T(8,128)(2,1)} %bitcast.20, bf16[768,384]{1,0:T(8,128)(2,1)} %bitcast.23, bf16[384,768]{1,0:T(8,128)(2,1)} %bitcast.25), custom_call_target="tpu_custom_call" | custom-call | tf_op jit(solution)/shard_map/weight_grads/pallas_call | solution.py:210
  132.1 63.1 %reduce-scatter.2.cloned.1.call-done.rows = bf16[256,768]{1,0:T(8,128)(2,1)} async-done(((bf16[2048,768]{1,0:T(8,128)(2,1)}), bf16[256,768]{1,0:T(8,128)(2,1)}) %reduce-scatter.2.cloned.1.call-update) | async-done | bytes 393232 | tf_op jit(solution)/shard_map/reduce_scatter | solution.py:224
  195.1 0.0 copy-start.1
  195.1 1.0 copy-done.1
  196.1 0.3 restore.1
  196.4 0.1 reshape.35
  196.5 35.5 %all_to_all.11 = bf16[64,4,768]{2,1,0:T(4,128)(2,1)S(1)} all-to-all(bf16[64,4,768]{2,1,0:T(4,128)(2,1)S(1)} %reshape.35), channel_id=1, replica_groups={{0,1,2,3,4,5,6,7,8,9,10,11,12,13,14,15,16,17,18,19,20,21,22,23,24,25,26..., dimensions={0} | all-to-all | bytes 786432 | tf_op jit(solution)/shard_map/all_to_all | solution.py:175
  232.0 0.1 reshape.36.home
  232.1 0.0 copy-done
  232.1 0.0 copy-done.2
  232.1 0.0 copy-done.3
  232.1 0.0 copy-done.4
  232.1 0.0 copy-done.5
  232.1 1.1 pick.1
Async XLA Ops:
  7.2 187.9 %reduce-scatter.2.cloned.1.call-start = ((), (), s32[]{:S(2)}) async-start(), calls=%async_computation.3 | async-start | bytes 3538944 | tf_op jit(solution)/shard_map/reduce_scatter | solution.py:224
  123.5 108.5 %copy-start = (bf16[128,768]{1,0:T(8,128)(2,1)S(1)}, bf16[128,768]{1,0:T(8,128)(2,1)}, u32[]{:S(2)}) copy-start(bf16[128,768]{1,0:T(8,128)(2,1)} %out_grad.3) | copy-start | bytes 589828
  123.5 108.5 %copy-start.2 = (s32[128]{0:T(128)S(1)}, s32[128]{0:T(128)}, u32[]{:S(2)}) copy-start(s32[128]{0:T(128)} %param.9) | copy-start | bytes 1540
  123.6 108.5 %copy-start.3 = (s32[128]{0:T(128)S(1)}, s32[128]{0:T(128)}, u32[]{:S(2)}) copy-start(s32[128]{0:T(128)} %param.10) | copy-start | bytes 1540
  123.6 108.5 %copy-start.4 = (s32[128]{0:T(128)S(1)}, s32[128]{0:T(128)}, u32[]{:S(2)}) copy-start(s32[128]{0:T(128)} %param.11) | copy-start | bytes 1540
  123.6 108.5 %copy-start.5 = (f32[128]{0:T(128)S(1)}, f32[128]{0:T(128)}, u32[]{:S(2)}) copy-start(f32[128]{0:T(128)} %param.12) | copy-start | bytes 1540
  195.1 1.0 copy-start.1
Sparse Core Ops, SparseCore 0:
  123.7 71.4 reduce-scatter.1

commit v7 on v4

--- a/solution.py
+++ b/solution.py
@@ -13,6 +13,10 @@
 KINDS = 2
 TILE = EGRP * KINDS * CAP
 VMEM_BYTES = 60 * 1024 * 1024
+VMEM_SMALL = 8 * 1024 * 1024
+STEPS = 229.0
+OCTAVES = 140.0
+SMALLEST = 2.0**-126
 
 gelu_root = math.sqrt(2.0 / math.pi)
 gelu_cubic = 0.044715
@@ -75,54 +79,77 @@
     token_grad[...] = dot((at == row + CAP).astype(jnp.bfloat16), home[...]).astype(jnp.bfloat16)
 
 
-def row_order(wide, transposed):
-    half = wide // TILE * CAP
+def row_order(wide, kind_first, transposed):
+    part_rows = wide // TILE * CAP
     shape = (wide, wide)
     index = lax.broadcasted_iota(jnp.int32, shape, 1 if transposed else 0)
     at = lax.broadcasted_iota(jnp.int32, shape, 0 if transposed else 1)
-    part = sum((index >= half * k).astype(jnp.int32) for k in range(1, EGRP * KINDS))
-    within = index - part * half
+    part = sum((index >= part_rows * k).astype(jnp.int32) for k in range(1, EGRP * KINDS))
+    within = index - part * part_rows
+    if kind_first:
+        part = (part & 1) * KINDS + (part >> 1)
     return (at == (within >> 1) * TILE + part * CAP + (within & 1)).astype(jnp.bfloat16)
 
 
-def order_kernel(transposed, rows, ordered):
-    ordered[...] = dot(row_order(rows.shape[0], transposed), rows[...]).astype(jnp.bfloat16)
-
-
-def forward_rows(rows, weight_in, weight_out):
-    sources, narrow, width = rows.shape
-    half = narrow // KINDS
-    rows_x = rows[:, :half, :].reshape(sources * half, width)
-    rows_g = rows[:, half:, :].reshape(sources * half, width)
-    pre_act = dot(rows_x, weight_in[...])
-    hidden_grad = dot(rows_g, weight_out[...], ((1,), (1,)))
-    value, slope = gelu_and_slope(pre_act)
-    return rows_x, rows_g, value.astype(jnp.bfloat16), (hidden_grad * slope).astype(jnp.bfloat16)
-
-
-def expert_kernel(group_ref, rows, weight_in, weight_out, send):
-    sources, narrow, width = rows.shape
-    half = narrow // KINDS
-    _, _, hidden, pre_grad = forward_rows(rows, weight_in, weight_out)
-    part_out = dot(hidden, weight_out[...]).astype(jnp.bfloat16)
-    part_in = dot(pre_grad, weight_in[...], ((1,), (1,))).astype(jnp.bfloat16)
-    own = pl.multiple_of(group_ref[0] * narrow, narrow)
-    other = pl.multiple_of((EGRP - 1 - group_ref[0]) * narrow, narrow)
-    send[:, pl.ds(other, narrow), :] = jnp.zeros((sources, narrow, width), jnp.bfloat16)
-    send[:, pl.ds(own, half), :] = part_out.reshape(sources, half, width)
-    send[:, pl.ds(own + half, half), :] = part_in.reshape(sources, half, width)
-
-
-def weights_kernel(group_ref, rows, weight_in, weight_out, grad_in, grad_out, sum_in, sum_out):
-    rows_x, rows_g, hidden, pre_grad = forward_rows(rows, weight_in, weight_out)
+def encode(value):
+    size = jnp.abs(value)
+    code = jnp.round((jnp.log2(jnp.maximum(size, SMALLEST)) + OCTAVES) * STEPS)
+    code = jnp.where(size < SMALLEST, 0.0, code)
+    return jnp.where(value < 0.0, -code, code).astype(jnp.int32).astype(jnp.int16)
+
+
+def decode(code):
+    wide = code.astype(jnp.int32).astype(jnp.float32)
+    value = jnp.exp2(jnp.abs(wide) * (1.0 / STEPS) - OCTAVES)
+    return jnp.where(wide < 0.0, -value, value).astype(jnp.bfloat16)
+
+
+def order_kernel(rows, codes_x, rows_g):
+    moved = dot(row_order(rows.shape[0], True, False), rows[...])
+    half = rows.shape[0] // KINDS
+    codes_x[...] = encode(moved[:half])
+    rows_g[...] = moved[half:].astype(jnp.bfloat16)
+
+
+def restore_kernel(rows, restored):
+    restored[...] = dot(row_order(rows.shape[0], False, True), rows[...]).astype(jnp.bfloat16)
+
+
+def flat(rows):
+    sources, count, width = rows.shape
+    return rows.reshape(sources * count, width)
+
+
+def activation_kernel(group_ref, codes_x, weight_in, weight_out, send, slopes):
+    sources, part, width = codes_x.shape
+    value, slope = gelu_and_slope(dot(flat(decode(codes_x[...])), weight_in[...]))
+    slopes[...] = slope
+    part_out = dot(value.astype(jnp.bfloat16), weight_out[...]).astype(jnp.bfloat16)
+    own = pl.multiple_of(group_ref[0] * (KINDS * part), part)
+    send[...] = jnp.zeros(send.shape, jnp.bfloat16)
+    send[:, pl.ds(own, part), :] = part_out.reshape(sources, part, width)
+
+
+def gradient_kernel(group_ref, rows_g, slopes, weight_in, weight_out, begun, send):
+    hidden_grad = dot(flat(rows_g[...]), weight_out[...], ((1,), (1,)))
+    pre_grad = (hidden_grad * slopes[...]).astype(jnp.bfloat16)
+    send[...] = dot(pre_grad, weight_in[...], ((1,), (1,))).astype(jnp.bfloat16).reshape(send.shape)
+
+
+def weights_kernel(group_ref, codes_x, rows_g, weight_in, weight_out, grad_in, grad_out, sum_in, sum_out):
+    x = flat(decode(codes_x[...]))
+    g = flat(rows_g[...])
+    value, slope = gelu_and_slope(dot(x, weight_in[...]))
+    hidden = value.astype(jnp.bfloat16)
+    pre_grad = (dot(g, weight_out[...], ((1,), (1,))) * slope).astype(jnp.bfloat16)
 
     @pl.when(pl.program_id(0) == 0)
     def _():
         sum_in[...] = jnp.zeros_like(sum_in)
         sum_out[...] = jnp.zeros_like(sum_out)
 
-    sum_in[...] += dot(rows_x, pre_grad, ((0,), (0,)))
-    sum_out[...] += dot(hidden, rows_g, ((0,), (0,)))
+    sum_in[...] += dot(x, pre_grad, ((0,), (0,)))
+    sum_out[...] += dot(hidden, g, ((0,), (0,)))
 
     @pl.when(pl.program_id(0) == pl.num_programs(0) - 1)
     def _():
@@ -141,6 +168,7 @@
     hidden_units = weight_in.shape[1]
     wide = intra_size * TILE
     params = pltpu.CompilerParams(vmem_limit_bytes=VMEM_BYTES)
+    small = pltpu.CompilerParams(vmem_limit_bytes=VMEM_SMALL)
     routing = (expert_ids[None], slot_ids[None], keep_mask[None], gate_prob[None])
 
     placed = pl.pallas_call(
@@ -150,55 +178,81 @@
         name="place",
     )(tokens, *routing, out_grad)
     moved = lax.all_to_all(placed.reshape(intra_size, TILE, width), "intra", 0, 0, tiled=True)
-
-    def reorder(rows, transposed, name):
-        return pl.pallas_call(
-            functools.partial(order_kernel, transposed),
-            out_shape=jax.ShapeDtypeStruct((wide, width), jnp.bfloat16),
-            compiler_params=params,
-            name=name,
-        )(rows.reshape(wide, width))
-
-    ordered = reorder(moved, False, "order")
-    spread = lax.all_gather(ordered[None], "inter", axis=0, tiled=True)
+    part = wide // (EGRP * KINDS)
+    ordered_x, ordered_g = pl.pallas_call(
+        order_kernel,
+        out_shape=[
+            jax.ShapeDtypeStruct((EGRP * part, width), jnp.int16),
+            jax.ShapeDtypeStruct((EGRP * part, width), jnp.bfloat16),
+        ],
+        compiler_params=small,
+        name="order",
+    )(moved.reshape(wide, width))
+    spread_g = lax.all_gather(ordered_g[None], "inter", axis=0, tiled=True)
+    spread_x = lax.all_gather(ordered_x[None], "inter", axis=0, tiled=True)
 
     step = 4
-    narrow = wide // EGRP
-    whole = lambda i, *_: (0, 0)
-    by_plane = pl.BlockSpec((step, wide, width), lambda i, *_: (i, 0, 0))
+    rows_all = inter_size * part
+    whole = lambda i, group_ref: (0, 0)
+    by_plane = pl.BlockSpec((step, wide, width), lambda i, group_ref: (i, 0, 0))
+    own_rows = pl.BlockSpec((step, part, width), lambda i, group_ref: (i, group_ref[0], 0))
+    own_gradients = pl.BlockSpec((step, part, width), lambda i, group_ref: (i, group_ref[0] * KINDS + 1, 0))
+    by_row = pl.BlockSpec((step * part, hidden_units), lambda i, group_ref: (i, 0))
     in_block = pl.BlockSpec((width, hidden_units), whole)
     out_block = pl.BlockSpec((hidden_units, width), whole)
-    own_rows = pl.BlockSpec((step, narrow, width), lambda i, group_ref: (i, group_ref[0], 0))
-
-    def over_planes(kernel, name, out_specs, out_shape, scratch):
+    send_shape = jax.ShapeDtypeStruct((inter_size, wide, width), jnp.bfloat16)
+
+    def over_planes(kernel, name, in_specs, out_specs, out_shape, operands, scratch=(), aliases={}):
         return pl.pallas_call(
             kernel,
             grid_spec=pltpu.PrefetchScalarGridSpec(
                 num_scalar_prefetch=1,
                 grid=(inter_size // step,),
-                in_specs=[own_rows, in_block, out_block],
+                in_specs=in_specs,
                 out_specs=out_specs,
                 scratch_shapes=scratch,
             ),
             out_shape=out_shape,
+            input_output_aliases=aliases,
             compiler_params=params,
             name=name,
-        )(group, spread, weight_in, weight_out)
-
+        )(group, *operands)
+
+    begun, slopes = over_planes(
+        activation_kernel,
+        "activations",
+        [own_rows, in_block, out_block],
+        [by_plane, by_row],
+        [send_shape, jax.ShapeDtypeStruct((rows_all, hidden_units), jnp.float32)],
+        (spread_x, weight_in, weight_out),
+    )
     send = over_planes(
-        expert_kernel, "expert", by_plane, jax.ShapeDtypeStruct((inter_size, wide, width), jnp.bfloat16), []
+        gradient_kernel,
+        "gradients",
+        [own_rows, by_row, in_block, out_block, pl.BlockSpec(memory_space=pl.ANY)],
+        own_gradients,
+        send_shape,
+        (spread_g, slopes, weight_in, weight_out, begun),
+        aliases={5: 0},
     )
     summed = lax.psum_scatter(send, "inter", scatter_dimension=0, tiled=True)
     in_weight_grad, out_weight_grad = over_planes(
         weights_kernel,
         "weight_grads",
+        [own_rows, own_rows, in_block, out_block],
         [in_block, out_block],
         [jax.ShapeDtypeStruct(w.shape, jnp.bfloat16) for w in (weight_in, weight_out)],
-        [pltpu.VMEM(w.shape, jnp.float32) for w in (weight_in, weight_out)],
+        (spread_x, spread_g, weight_in, weight_out),
+        scratch=[pltpu.VMEM(w.shape, jnp.float32) for w in (weight_in, weight_out)],
     )
     summed, out_weight_grad, in_weight_grad = lax.optimization_barrier((summed, out_weight_grad, in_weight_grad))
 
-    back = reorder(summed, True, "restore")
+    back = pl.pallas_call(
+        restore_kernel,
+        out_shape=jax.ShapeDtypeStruct((wide, width), jnp.bfloat16),
+        compiler_params=small,
+        name="restore",
+    )(summed.reshape(wide, width))
     home = lax.all_to_all(back.reshape(intra_size, TILE, width), "intra", 0, 0, tiled=True)
     expert_out, gate_grad, token_grad = pl.pallas_call(
         functools.partial(pick_kernel, intra_size),
@@ -207,7 +261,7 @@
             jax.ShapeDtypeStruct((1, tok_rows), jnp.float32),
             jax.ShapeDtypeStruct((tok_rows, width), jnp.bfloat16),
         ],
-        compiler_params=pltpu.CompilerParams(vmem_limit_bytes=16 * 1024 * 1024),
+        compiler_params=small,
         name="pick",
     )(home.reshape(wide, width), *routing, out_grad)
     return (

time: 238 us -> 235 us (0.987)
  waiting for transfers between devices: 155 us -> 75.5 us
  blocking collectives: 45.9 us -> 118 us
  Pallas kernels: 22.6 us -> 25.1 us
    all_gather x1, waiting for transfers between devices: 82.2 us -> 0.01 us  [on_device(): spread_g = lax.all_gather(ordered_g[None], 'inter', axis=0, tiled=True)]
    all_gather x0 -> x1, blocking collectives: none -> 73.7 us  [on_device(): spread_x = lax.all_gather(ordered_x[None], 'inter', axis=0, tiled=True)]
    pallas_call x2 -> x3, Pallas kernels: 15.2 us -> 20.4 us  [over_planes(): pl.pallas_call(kernel, grid_spec=pltpu.PrefetchScalarGridSpec(num_scalar_...]
    reduce_scatter x1, waiting for transfers between devices: 72.3 us -> 75.5 us  [on_device(): summed = lax.psum_scatter(send, 'inter', scatter_dimension=0, tiled=True)]
    pallas_call x2, Pallas kernels: 4.02 us -> 1.29 us  [the longest x1 1.03 us: on_device(): pl.pallas_call(order_kernel, out_shape=[jax.ShapeDtypeStruct((EGRP * part...]
  transfers between devices with their start and end apart: 2 -> 2, of which waited for: 2 -> 1; matrix products, arithmetic and copies ran while one was open for 0% -> 0% of each run, Pallas kernels for 3% -> 6%
where the time goes in v7:
time: 235 us; the launch traced here: 234 us
  blocking collectives  118 us (50%)
  waiting for transfers between devices  75.5 us (32%)
  Pallas kernels  25.1 us (11%)
  between operations  14.1 us (6%)
    reduce_scatter x1, waiting for transfers between devices, on_device(): summed = lax.psum_scatter(send, 'inter', scatter_dimension=0, tiled=True)  75.5 us
    all_gather x1, blocking collectives, on_device(): spread_x = lax.all_gather(ordered_x[None], 'inter', axis=0, tiled=True)  73.7 us
    all_to_all x1, blocking collectives, on_device(): lax.all_to_all(back.reshape(intra_size, TILE, width), 'intra', 0, 0, tile...  24.1 us
    all_to_all x1, blocking collectives, on_device(): lax.all_to_all(placed.reshape(intra_size, TILE, width), 'intra', 0, 0, ti...  20.7 us
    pallas_call x3, Pallas kernels, over_planes(): pl.pallas_call(kernel, grid_spec=pltpu.PrefetchScalarGridSpec(num_scalar_...  20.4 us
  transfers between devices with their start and end apart: 2, of which 1 were waited for; matrix products, arithmetic and copies ran while one was open for 0% of the time, Pallas kernels for 6%

profile of v7, /device:TPU:1, one launch (start us, length us, event | category | flops | bytes accessed | tf_op | source)
XLA Modules:
  0.0 234.3 jit_solution(17761861406429870168)
XLA Ops:
  7.2 0.0 all-gather.5.cloned.1.call-start
  7.2 2.3 place.1
  9.5 20.7 %all_to_all.10 = bf16[32,8,768]{2,1,0:T(8,128)(2,1)S(1)} all-to-all(bf16[32,8,768]{2,1,0:T(8,128)(2,1)} %bitcast.39), channel_id=1, replica_groups=mesh['inter'=16,'intra'=32] {'intra'}, dimensions={0} | all-to-all | bytes 786432 | tf_op jit(solution)/shard_map/all_to_all | solution.py:180
  30.2 1.0 order.1
  31.2 0.0 all-gather.5.cloned.1.call-update
  31.2 0.0 reduce-scatter.2.cloned.1.call-start
  31.3 73.7 %all-gather.6 = s16[2048,768]{1,0:T(8,128)(2,1)} all-gather(s16[128,768]{1,0:T(8,128)(2,1)S(1)} %get-tuple-element.18), channel_id=3, replica_groups=mesh['inter'=16,'intra'=32] {'inter'}, dimensions={0}, use_global_device_ids=true | all-gather | bytes 3342336 | tf_op jit(solution)/shard_map/all_gather | solution.py:192
  104.9 6.6 %activations.1 = (bf16[16,256,768]{2,1,0:T(8,128)(2,1)}, f32[1024,384]{1,0:T(8,128)}) custom-call(s32[1]{0:T(128)} %bitcast.group_ref, s16[16,128,768]{2,1,0:T(8,128)(2,1)} %bitcast.29, bf16[768,384]{1,0:T(8,128)(2,1)} %bitcast.33, bf16[384,768]{1,0:T(8,128)(2,1)} %bitcast.36), custom_call_target="tpu_custom_call" | custom-call | tf_op jit(solution)/shard_map/activations/pallas_call | solution.py:206
  111.5 0.0 all-gather.5.cloned.1.call-done
  111.5 5.7 %gradients.1 = bf16[16,256,768]{2,1,0:T(8,128)(2,1)} custom-call(s32[1]{0:T(128)} %bitcast.group_ref, bf16[16,128,768]{2,1,0:T(8,128)(2,1)} %bitcast.31, f32[1024,384]{1,0:T(8,128)} %get-tuple-element.19.slopes, bf16[768,384]{1,0:T(8,128)(2,1)} %bitcast.34, bf16[384,768]{1,0:T(8,128)(2,1)} %bitcast.37, ...), custom_call_target="tpu_custom_call", output_to_operand_aliasing={{}: (5, {})} | custom-call | tf_op jit(solution)/shard_map/gradients/pallas_call | solution.py:206
  117.2 0.0 reduce-scatter.2.cloned.1.call-update
  117.2 0.0 copy-start
  117.3 0.0 copy-start.2
  117.3 0.0 copy-start.3
  117.3 0.0 copy-start.4
  117.3 0.0 copy-start.5
  117.3 8.1 %weight_grads.1 = (bf16[768,384]{1,0:T(8,128)(2,1)}, bf16[384,768]{1,0:T(8,128)(2,1)}) custom-call(s32[1]{0:T(128)} %bitcast.group_ref, s16[16,128,768]{2,1,0:T(8,128)(2,1)} %bitcast.30, bf16[16,128,768]{2,1,0:T(8,128)(2,1)} %bitcast.32, bf16[768,384]{1,0:T(8,128)(2,1)} %bitcast.35, bf16[384,768]{1,0:T(8,128)(2,1)} %bitcast.38), custom_call_target="tpu_custom_call" | custom-call | tf_op jit(solution)/shard_map/weight_grads/pallas_call | solution.py:206
  125.4 75.5 %reduce-scatter.2.cloned.1.call-done = bf16[1,256,768]{2,1,0:T(8,128)(2,1)} async-done(((bf16[16,256,768]{2,1,0:T(8,128)(2,1)}), bf16[1,256,768]{2,1,0:T(8,128)(2,1)}) %reduce-scatter.2.cloned.1.call-update) | async-done | bytes 393232 | tf_op jit(solution)/shard_map/reduce_scatter | solution.py:238
  200.9 0.0 copy-start.1
  200.9 1.0 copy-done.1
  201.9 0.3 restore.1
  202.1 24.1 %all_to_all.11 = bf16[32,8,768]{2,1,0:T(8,128)(2,1)S(1)} all-to-all(bf16[32,8,768]{2,1,0:T(8,128)(2,1)S(1)} %bitcast.19), channel_id=1, replica_groups=mesh['inter'=16,'intra'=32] {'intra'}, dimensions={0} | all-to-all | bytes 786432 | tf_op jit(solution)/shard_map/all_to_all | solution.py:256
  226.3 0.0 copy-done
  226.3 0.0 copy-done.2
  226.3 0.0 copy-done.3
  226.3 0.0 copy-done.4
  226.3 0.0 copy-done.5
  226.3 1.1 pick.1
Async XLA Ops:
  7.2 104.3 %all-gather.5.cloned.1.call-start = ((), (), s32[]{:S(2)}) async-start(), calls=%async_computation.4 | async-start | bytes 3342336 | tf_op jit(solution)/shard_map/all_gather | solution.py:191
  31.2 169.7 %reduce-scatter.2.cloned.1.call-start = ((), (), s32[]{:S(2)}) async-start(), calls=%async_computation.3 | async-start | bytes 6684672 | tf_op jit(solution)/shard_map/reduce_scatter | solution.py:238
  117.2 109.0 %copy-start = (bf16[128,768]{1,0:T(8,128)(2,1)S(1)}, bf16[128,768]{1,0:T(8,128)(2,1)}, u32[]{:S(2)}) copy-start(bf16[128,768]{1,0:T(8,128)(2,1)} %out_grad.3) | copy-start | bytes 589828
  117.3 109.0 %copy-start.2 = (s32[128]{0:T(128)S(1)}, s32[128]{0:T(128)}, u32[]{:S(2)}) copy-start(s32[128]{0:T(128)} %param.9) | copy-start | bytes 1540
  117.3 109.0 %copy-start.3 = (s32[128]{0:T(128)S(1)}, s32[128]{0:T(128)}, u32[]{:S(2)}) copy-start(s32[128]{0:T(128)} %param.10) | copy-start | bytes 1540
  117.3 109.0 %copy-start.4 = (s32[128]{0:T(128)S(1)}, s32[128]{0:T(128)}, u32[]{:S(2)}) copy-start(s32[128]{0:T(128)} %param.11) | copy-start | bytes 1540
  117.3 109.0 %copy-start.5 = (f32[128]{0:T(128)S(1)}, f32[128]{0:T(128)}, u32[]{:S(2)}) copy-start(f32[128]{0:T(128)} %param.12) | copy-start | bytes 1540
  200.9 1.0 copy-start.1
Sparse Core Ops, SparseCore 0:
  31.3 77.1 all-gather.4
  117.4 83.4 reduce-scatter.1

commit v8 on v7

--- a/solution.py
+++ b/solution.py
@@ -120,36 +120,38 @@
     return rows.reshape(sources * count, width)
 
 
-def activation_kernel(group_ref, codes_x, weight_in, weight_out, send, slopes):
+def forward_rows(codes_x, rows_g, weight_in, weight_out):
+    rows_x = flat(decode(codes_x[...]))
+    rows_g = flat(rows_g[...])
+    pre_act = dot(rows_x, weight_in[...])
+    hidden_grad = dot(rows_g, weight_out[...], ((1,), (1,)))
+    value, slope = gelu_and_slope(pre_act)
+    return rows_x, rows_g, value.astype(jnp.bfloat16), (hidden_grad * slope).astype(jnp.bfloat16)
+
+
+def expert_kernel(group_ref, codes_x, rows_g, weight_in, weight_out, send):
     sources, part, width = codes_x.shape
-    value, slope = gelu_and_slope(dot(flat(decode(codes_x[...])), weight_in[...]))
-    slopes[...] = slope
-    part_out = dot(value.astype(jnp.bfloat16), weight_out[...]).astype(jnp.bfloat16)
-    own = pl.multiple_of(group_ref[0] * (KINDS * part), part)
-    send[...] = jnp.zeros(send.shape, jnp.bfloat16)
+    _, _, hidden, pre_grad = forward_rows(codes_x, rows_g, weight_in, weight_out)
+    part_out = dot(hidden, weight_out[...]).astype(jnp.bfloat16)
+    part_in = dot(pre_grad, weight_in[...], ((1,), (1,))).astype(jnp.bfloat16)
+    narrow = KINDS * part
+    own = pl.multiple_of(group_ref[0] * narrow, narrow)
+    other = pl.multiple_of((EGRP - 1 - group_ref[0]) * narrow, narrow)
+    send[:, pl.ds(other, narrow), :] = jnp.zeros((sources, narrow, width), jnp.bfloat16)
     send[:, pl.ds(own, part), :] = part_out.reshape(sources, part, width)
-
-
-def gradient_kernel(group_ref, rows_g, slopes, weight_in, weight_out, begun, send):
-    hidden_grad = dot(flat(rows_g[...]), weight_out[...], ((1,), (1,)))
-    pre_grad = (hidden_grad * slopes[...]).astype(jnp.bfloat16)
-    send[...] = dot(pre_grad, weight_in[...], ((1,), (1,))).astype(jnp.bfloat16).reshape(send.shape)
+    send[:, pl.ds(own + part, part), :] = part_in.reshape(sources, part, width)
 
 
 def weights_kernel(group_ref, codes_x, rows_g, weight_in, weight_out, grad_in, grad_out, sum_in, sum_out):
-    x = flat(decode(codes_x[...]))
-    g = flat(rows_g[...])
-    value, slope = gelu_and_slope(dot(x, weight_in[...]))
-    hidden = value.astype(jnp.bfloat16)
-    pre_grad = (dot(g, weight_out[...], ((1,), (1,))) * slope).astype(jnp.bfloat16)
+    rows_x, rows_g, hidden, pre_grad = forward_rows(codes_x, rows_g, weight_in, weight_out)
 
     @pl.when(pl.program_id(0) == 0)
     def _():
         sum_in[...] = jnp.zeros_like(sum_in)
         sum_out[...] = jnp.zeros_like(sum_out)
 
-    sum_in[...] += dot(x, pre_grad, ((0,), (0,)))
-    sum_out[...] += dot(hidden, g, ((0,), (0,)))
+    sum_in[...] += dot(rows_x, pre_grad, ((0,), (0,)))
+    sum_out[...] += dot(hidden, rows_g, ((0,), (0,)))
 
     @pl.when(pl.program_id(0) == pl.num_programs(0) - 1)
     def _():
@@ -192,58 +194,37 @@
     spread_x = lax.all_gather(ordered_x[None], "inter", axis=0, tiled=True)
 
     step = 4
-    rows_all = inter_size * part
     whole = lambda i, group_ref: (0, 0)
     by_plane = pl.BlockSpec((step, wide, width), lambda i, group_ref: (i, 0, 0))
     own_rows = pl.BlockSpec((step, part, width), lambda i, group_ref: (i, group_ref[0], 0))
-    own_gradients = pl.BlockSpec((step, part, width), lambda i, group_ref: (i, group_ref[0] * KINDS + 1, 0))
-    by_row = pl.BlockSpec((step * part, hidden_units), lambda i, group_ref: (i, 0))
     in_block = pl.BlockSpec((width, hidden_units), whole)
     out_block = pl.BlockSpec((hidden_units, width), whole)
-    send_shape = jax.ShapeDtypeStruct((inter_size, wide, width), jnp.bfloat16)
-
-    def over_planes(kernel, name, in_specs, out_specs, out_shape, operands, scratch=(), aliases={}):
+
+    def over_planes(kernel, name, out_specs, out_shape, scratch):
         return pl.pallas_call(
             kernel,
             grid_spec=pltpu.PrefetchScalarGridSpec(
                 num_scalar_prefetch=1,
                 grid=(inter_size // step,),
-                in_specs=in_specs,
+                in_specs=[own_rows, own_rows, in_block, out_block],
                 out_specs=out_specs,
                 scratch_shapes=scratch,
             ),
             out_shape=out_shape,
-            input_output_aliases=aliases,
             compiler_params=params,
             name=name,
-        )(group, *operands)
-
-    begun, slopes = over_planes(
-        activation_kernel,
-        "activations",
-        [own_rows, in_block, out_block],
-        [by_plane, by_row],
-        [send_shape, jax.ShapeDtypeStruct((rows_all, hidden_units), jnp.float32)],
-        (spread_x, weight_in, weight_out),
-    )
+        )(group, spread_x, spread_g, weight_in, weight_out)
+
     send = over_planes(
-        gradient_kernel,
-        "gradients",
-        [own_rows, by_row, in_block, out_block, pl.BlockSpec(memory_space=pl.ANY)],
-        own_gradients,
-        send_shape,
-        (spread_g, slopes, weight_in, weight_out, begun),
-        aliases={5: 0},
+        expert_kernel, "expert", by_plane, jax.ShapeDtypeStruct((inter_size, wide, width), jnp.bfloat16), []
     )
     summed = lax.psum_scatter(send, "inter", scatter_dimension=0, tiled=True)
     in_weight_grad, out_weight_grad = over_planes(
         weights_kernel,
         "weight_grads",
-        [own_rows, own_rows, in_block, out_block],
         [in_block, out_block],
         [jax.ShapeDtypeStruct(w.shape, jnp.bfloat16) for w in (weight_in, weight_out)],
-        (spread_x, spread_g, weight_in, weight_out),
-        scratch=[pltpu.VMEM(w.shape, jnp.float32) for w in (weight_in, weight_out)],
+        [pltpu.VMEM(w.shape, jnp.float32) for w in (weight_in, weight_out)],
     )
     summed, out_weight_grad, in_weight_grad = lax.optimization_barrier((summed, out_weight_grad, in_weight_grad))
 

time: 235 us -> 232 us (0.987)
  Pallas kernels: 25.1 us -> 20.3 us
    pallas_call x3 -> x2, Pallas kernels: 20.4 us -> 15.6 us  [over_planes(): pl.pallas_call(kernel, grid_spec=pltpu.PrefetchScalarGridSpec(num_scalar_...]
    all_gather x1, waiting for transfers between devices: 0.01 us -> 3.58 us  [on_device(): spread_g = lax.all_gather(ordered_g[None], 'inter', axis=0, tiled=True)]
  transfers between devices with their start and end apart: 2 -> 2, of which waited for: 1 -> 2; matrix products, arithmetic and copies ran while one was open for 0% -> 0% of each run, Pallas kernels for 6% -> 3%
where the time goes in v8:
time: 232 us
  blocking collectives  119 us (51%)
  waiting for transfers between devices  77.6 us (33%)
  Pallas kernels  20.3 us (9%)
  between operations  14.1 us (6%)
    reduce_scatter x1, waiting for transfers between devices, on_device(): summed = lax.psum_scatter(send, 'inter', scatter_dimension=0, tiled=True)  74 us
    all_gather x1, blocking collectives, on_device(): spread_x = lax.all_gather(ordered_x[None], 'inter', axis=0, tiled=True)  73.7 us
    all_to_all x1, blocking collectives, on_device(): lax.all_to_all(back.reshape(intra_size, TILE, width), 'intra', 0, 0, tile...  24.2 us
    all_to_all x1, blocking collectives, on_device(): lax.all_to_all(placed.reshape(intra_size, TILE, width), 'intra', 0, 0, ti...  20.7 us
    pallas_call x2, Pallas kernels, over_planes(): pl.pallas_call(kernel, grid_spec=pltpu.PrefetchScalarGridSpec(num_scalar_...  15.6 us
  transfers between devices with their start and end apart: 2, of which 2 were waited for; matrix products, arithmetic and copies ran while one was open for 0% of the time, Pallas kernels for 3%

profile of v8, /device:TPU:1, one launch (start us, length us, event | category | flops | bytes accessed | tf_op | source)
XLA Modules:
  0.0 231.6 jit_solution(4658604728015134041)
XLA Ops:
  7.2 0.0 all-gather.5.cloned.1.call-start
  7.2 2.3 place.1
  9.5 20.7 %all_to_all.10 = bf16[32,8,768]{2,1,0:T(8,128)(2,1)S(1)} all-to-all(bf16[32,8,768]{2,1,0:T(8,128)(2,1)} %bitcast.37), channel_id=1, replica_groups=mesh['inter'=16,'intra'=32] {'intra'}, dimensions={0} | all-to-all | bytes 786432 | tf_op jit(solution)/shard_map/all_to_all | solution.py:182
  30.2 1.0 order.1
  31.2 0.0 all-gather.5.cloned.1.call-update
  31.2 0.0 reduce-scatter.2.cloned.1.call-start
  31.3 73.7 %all-gather.6 = s16[2048,768]{1,0:T(8,128)(2,1)} all-gather(s16[128,768]{1,0:T(8,128)(2,1)S(1)} %get-tuple-element.15), channel_id=2, replica_groups=mesh['inter'=16,'intra'=32] {'inter'}, dimensions={0}, use_global_device_ids=true | all-gather | bytes 3342336 | tf_op jit(solution)/shard_map/all_gather | solution.py:194
  104.9 3.6 %all-gather.5.cloned.1.call-done = bf16[2048,768]{1,0:T(8,128)(2,1)} async-done(((bf16[128,768]{1,0:T(8,128)(2,1)}), bf16[2048,768]{1,0:T(8,128)(2,1)}) %all-gather.5.cloned.1.call-update) | async-done | bytes 3145744 | tf_op jit(solution)/shard_map/all_gather | solution.py:193
  108.5 7.5 %expert.1 = bf16[16,256,768]{2,1,0:T(8,128)(2,1)} custom-call(s32[1]{0:T(128)} %bitcast.group_ref, s16[16,128,768]{2,1,0:T(8,128)(2,1)} %bitcast.29, bf16[16,128,768]{2,1,0:T(8,128)(2,1)} %bitcast.31, bf16[768,384]{1,0:T(8,128)(2,1)} %bitcast.33, bf16[384,768]{1,0:T(8,128)(2,1)} %bitcast.35), custom_call_target="tpu_custom_call" | custom-call | tf_op jit(solution)/shard_map/expert/pallas_call | solution.py:204
  116.1 0.0 reduce-scatter.2.cloned.1.call-update
  116.1 0.0 copy-start
  116.1 0.0 copy-start.2
  116.1 0.0 copy-start.3
  116.1 0.0 copy-start.4
  116.1 0.0 copy-start.5
  116.2 8.1 %weight_grads.1 = (bf16[768,384]{1,0:T(8,128)(2,1)}, bf16[384,768]{1,0:T(8,128)(2,1)}) custom-call(s32[1]{0:T(128)} %bitcast.group_ref, s16[16,128,768]{2,1,0:T(8,128)(2,1)} %bitcast.30, bf16[16,128,768]{2,1,0:T(8,128)(2,1)} %bitcast.32, bf16[768,384]{1,0:T(8,128)(2,1)} %bitcast.34, bf16[384,768]{1,0:T(8,128)(2,1)} %bitcast.36), custom_call_target="tpu_custom_call" | custom-call | tf_op jit(solution)/shard_map/weight_grads/pallas_call | solution.py:204
  124.2 74.0 %reduce-scatter.2.cloned.1.call-done = bf16[1,256,768]{2,1,0:T(8,128)(2,1)} async-done(((bf16[16,256,768]{2,1,0:T(8,128)(2,1)}), bf16[1,256,768]{2,1,0:T(8,128)(2,1)}) %reduce-scatter.2.cloned.1.call-update) | async-done | bytes 393232 | tf_op jit(solution)/shard_map/reduce_scatter | solution.py:221
  198.2 0.0 copy-start.1
  198.2 1.0 copy-done.1
  199.2 0.3 restore.1
  199.4 24.2 %all_to_all.11 = bf16[32,8,768]{2,1,0:T(8,128)(2,1)S(1)} all-to-all(bf16[32,8,768]{2,1,0:T(8,128)(2,1)S(1)} %bitcast.19), channel_id=1, replica_groups=mesh['inter'=16,'intra'=32] {'intra'}, dimensions={0} | all-to-all | bytes 786432 | tf_op jit(solution)/shard_map/all_to_all | solution.py:237
  223.6 0.0 copy-done
  223.6 0.0 copy-done.2
  223.6 0.0 copy-done.3
  223.6 0.0 copy-done.4
  223.6 0.0 copy-done.5
  223.7 1.1 pick.1
Async XLA Ops:
  7.2 101.4 %all-gather.5.cloned.1.call-start = ((), (), s32[]{:S(2)}) async-start(), calls=%async_computation.4 | async-start | bytes 3342336 | tf_op jit(solution)/shard_map/all_gather | solution.py:193
  31.2 167.0 %reduce-scatter.2.cloned.1.call-start = ((), (), s32[]{:S(2)}) async-start(), calls=%async_computation.3 | async-start | bytes 6684672 | tf_op jit(solution)/shard_map/reduce_scatter | solution.py:221
  116.1 107.5 %copy-start = (bf16[128,768]{1,0:T(8,128)(2,1)S(1)}, bf16[128,768]{1,0:T(8,128)(2,1)}, u32[]{:S(2)}) copy-start(bf16[128,768]{1,0:T(8,128)(2,1)} %out_grad.3) | copy-start | bytes 589828
  116.1 107.5 %copy-start.2 = (s32[128]{0:T(128)S(1)}, s32[128]{0:T(128)}, u32[]{:S(2)}) copy-start(s32[128]{0:T(128)} %param.9) | copy-start | bytes 1540
  116.1 107.5 %copy-start.3 = (s32[128]{0:T(128)S(1)}, s32[128]{0:T(128)}, u32[]{:S(2)}) copy-start(s32[128]{0:T(128)} %param.10) | copy-start | bytes 1540
  116.1 107.5 %copy-start.4 = (s32[128]{0:T(128)S(1)}, s32[128]{0:T(128)}, u32[]{:S(2)}) copy-start(s32[128]{0:T(128)} %param.11) | copy-start | bytes 1540
  116.1 107.5 %copy-start.5 = (f32[128]{0:T(128)S(1)}, f32[128]{0:T(128)}, u32[]{:S(2)}) copy-start(f32[128]{0:T(128)} %param.12) | copy-start | bytes 1540
  198.2 1.0 copy-start.1
Sparse Core Ops, SparseCore 0:
  31.3 77.1 all-gather.4
  116.2 81.9 reduce-scatter.1

commit v9 on v8

--- a/solution.py
+++ b/solution.py
@@ -14,6 +14,7 @@
 TILE = EGRP * KINDS * CAP
 VMEM_BYTES = 60 * 1024 * 1024
 VMEM_SMALL = 8 * 1024 * 1024
+TAIL = 128
 STEPS = 229.0
 OCTAVES = 140.0
 SMALLEST = 2.0**-126
@@ -104,11 +105,16 @@
     return jnp.where(wide < 0.0, -value, value).astype(jnp.bfloat16)
 
 
-def order_kernel(rows, codes_x, rows_g):
-    moved = dot(row_order(rows.shape[0], True, False), rows[...])
-    half = rows.shape[0] // KINDS
-    codes_x[...] = encode(moved[:half])
-    rows_g[...] = moved[half:].astype(jnp.bfloat16)
+def order_gradients_kernel(rows, rows_g):
+    order = row_order(rows.shape[0], True, False)[rows.shape[0] // KINDS :]
+    rows_g[...] = dot(order, rows[:, : rows_g.shape[1]]).astype(jnp.bfloat16)
+
+
+def order_codes_kernel(rows, codes):
+    count, width = rows.shape
+    moved = dot(row_order(count, True, False), rows[...])
+    codes[:, :width] = encode(moved[: count // KINDS])
+    codes[:, width:] = encode(moved[count // KINDS :, width - TAIL :])
 
 
 def restore_kernel(rows, restored):
@@ -120,18 +126,21 @@
     return rows.reshape(sources * count, width)
 
 
-def forward_rows(codes_x, rows_g, weight_in, weight_out):
-    rows_x = flat(decode(codes_x[...]))
-    rows_g = flat(rows_g[...])
+def forward_rows(codes, rows_g, weight_in, weight_out):
+    width = weight_in.shape[0]
+    decoded = decode(flat(codes[...]))
+    rows_x = decoded[:, :width]
+    rows_g = jnp.concatenate([flat(rows_g[...]), decoded[:, width:]], axis=1)
     pre_act = dot(rows_x, weight_in[...])
     hidden_grad = dot(rows_g, weight_out[...], ((1,), (1,)))
     value, slope = gelu_and_slope(pre_act)
     return rows_x, rows_g, value.astype(jnp.bfloat16), (hidden_grad * slope).astype(jnp.bfloat16)
 
 
-def expert_kernel(group_ref, codes_x, rows_g, weight_in, weight_out, send):
-    sources, part, width = codes_x.shape
-    _, _, hidden, pre_grad = forward_rows(codes_x, rows_g, weight_in, weight_out)
+def expert_kernel(group_ref, codes, rows_g, weight_in, weight_out, send):
+    sources, part, _ = codes.shape
+    width = send.shape[2]
+    _, _, hidden, pre_grad = forward_rows(codes, rows_g, weight_in, weight_out)
     part_out = dot(hidden, weight_out[...]).astype(jnp.bfloat16)
     part_in = dot(pre_grad, weight_in[...], ((1,), (1,))).astype(jnp.bfloat16)
     narrow = KINDS * part
@@ -142,8 +151,8 @@
     send[:, pl.ds(own + part, part), :] = part_in.reshape(sources, part, width)
 
 
-def weights_kernel(group_ref, codes_x, rows_g, weight_in, weight_out, grad_in, grad_out, sum_in, sum_out):
-    rows_x, rows_g, hidden, pre_grad = forward_rows(codes_x, rows_g, weight_in, weight_out)
+def weights_kernel(group_ref, codes, rows_g, weight_in, weight_out, grad_in, grad_out, sum_in, sum_out):
+    rows_x, rows_g, hidden, pre_grad = forward_rows(codes, rows_g, weight_in, weight_out)
 
     @pl.when(pl.program_id(0) == 0)
     def _():
@@ -181,22 +190,25 @@
     )(tokens, *routing, out_grad)
     moved = lax.all_to_all(placed.reshape(intra_size, TILE, width), "intra", 0, 0, tiled=True)
     part = wide // (EGRP * KINDS)
-    ordered_x, ordered_g = pl.pallas_call(
-        order_kernel,
-        out_shape=[
-            jax.ShapeDtypeStruct((EGRP * part, width), jnp.int16),
-            jax.ShapeDtypeStruct((EGRP * part, width), jnp.bfloat16),
-        ],
-        compiler_params=small,
-        name="order",
-    )(moved.reshape(wide, width))
+    half = EGRP * part
+
+    def order(kernel, name, columns, dtype):
+        return pl.pallas_call(
+            kernel,
+            out_shape=jax.ShapeDtypeStruct((half, columns), dtype),
+            compiler_params=small,
+            name=name,
+        )(moved.reshape(wide, width))
+
+    ordered_g = order(order_gradients_kernel, "order_gradients", width - TAIL, jnp.bfloat16)
+    ordered_x = order(order_codes_kernel, "order_codes", width + TAIL, jnp.int16)
     spread_g = lax.all_gather(ordered_g[None], "inter", axis=0, tiled=True)
     spread_x = lax.all_gather(ordered_x[None], "inter", axis=0, tiled=True)
 
     step = 4
     whole = lambda i, group_ref: (0, 0)
     by_plane = pl.BlockSpec((step, wide, width), lambda i, group_ref: (i, 0, 0))
-    own_rows = pl.BlockSpec((step, part, width), lambda i, group_ref: (i, group_ref[0], 0))
+    own = lambda columns: pl.BlockSpec((step, part, columns), lambda i, group_ref: (i, group_ref[0], 0))
     in_block = pl.BlockSpec((width, hidden_units), whole)
     out_block = pl.BlockSpec((hidden_units, width), whole)
 
@@ -206,7 +218,7 @@
             grid_spec=pltpu.PrefetchScalarGridSpec(
                 num_scalar_prefetch=1,
                 grid=(inter_size // step,),
-                in_specs=[own_rows, own_rows, in_block, out_block],
+                in_specs=[own(width + TAIL), own(width - TAIL), in_block, out_block],
                 out_specs=out_specs,
                 scratch_shapes=scratch,
             ),

time: 232 us -> 231 us (level)
  waiting for transfers between devices: 77.6 us -> 68.6 us
  blocking collectives: 119 us -> 126 us
    all_gather x1, blocking collectives: 73.7 us -> 80.9 us  [on_device(): spread_x = lax.all_gather(ordered_x[None], 'inter', axis=0, tiled=True)]
    reduce_scatter x1, waiting for transfers between devices: 74 us -> 68.6 us  [on_device(): summed = lax.psum_scatter(send, 'inter', scatter_dimension=0, tiled=True)]
    all_gather x1, waiting for transfers between devices: 3.58 us -> 0.01 us  [on_device(): spread_g = lax.all_gather(ordered_g[None], 'inter', axis=0, tiled=True)]
  transfers between devices with their start and end apart: 2 -> 2, of which waited for: 2 -> 1; matrix products, arithmetic and copies ran while one was open for 0% -> 0% of each run, Pallas kernels for 3% -> 4%
where the time goes in v9:
time: 231 us; the launch traced here: 230 us
  blocking collectives  126 us (55%)
  waiting for transfers between devices  68.6 us (30%)
  Pallas kernels  20.6 us (9%)
  between operations  14.1 us (6%)
    all_gather x1, blocking collectives, on_device(): spread_x = lax.all_gather(ordered_x[None], 'inter', axis=0, tiled=True)  80.9 us
    reduce_scatter x1, waiting for transfers between devices, on_device(): summed = lax.psum_scatter(send, 'inter', scatter_dimension=0, tiled=True)  68.6 us
    all_to_all x1, blocking collectives, on_device(): lax.all_to_all(back.reshape(intra_size, TILE, width), 'intra', 0, 0, tile...  24 us
    all_to_all x1, blocking collectives, on_device(): lax.all_to_all(placed.reshape(intra_size, TILE, width), 'intra', 0, 0, ti...  20.7 us
    pallas_call x2, Pallas kernels, over_planes(): pl.pallas_call(kernel, grid_spec=pltpu.PrefetchScalarGridSpec(num_scalar_...  15.7 us
  transfers between devices with their start and end apart: 2, of which 1 were waited for; matrix products, arithmetic and copies ran while one was open for 0% of the time, Pallas kernels for 4%

profile of v9, /device:TPU:1, one launch (start us, length us, event | category | flops | bytes accessed | tf_op | source)
XLA Modules:
  0.0 230.1 jit_solution(3758541961775632734)
XLA Ops:
  7.2 0.0 all-gather.5.cloned.1.call-start
  7.2 2.3 place.1
  9.5 20.7 %all_to_all.10 = bf16[32,8,768]{2,1,0:T(8,128)(2,1)S(1)} all-to-all(bf16[32,8,768]{2,1,0:T(8,128)(2,1)} %bitcast.38), channel_id=1, replica_groups=mesh['inter'=16,'intra'=32] {'intra'}, dimensions={0} | all-to-all | bytes 786432 | tf_op jit(solution)/shard_map/all_to_all | solution.py:191
  30.2 0.9 order_gradients.1
  31.0 0.0 all-gather.5.cloned.1.call-update
  31.1 0.0 reduce-scatter.2.cloned.1.call-start
  31.1 0.4 order_codes.1
  31.5 80.9 %all-gather.6 = s16[2048,896]{1,0:T(8,128)(2,1)} all-gather(s16[128,896]{1,0:T(8,128)(2,1)S(1)} %order_codes.1), channel_id=2, replica_groups=mesh['inter'=16,'intra'=32] {'inter'}, dimensions={0}, use_global_device_ids=true | all-gather | bytes 3899392 | tf_op jit(solution)/shard_map/all_gather | solution.py:206
  112.5 0.0 all-gather.5.cloned.1.call-done
  112.5 7.6 %expert.1 = bf16[16,256,768]{2,1,0:T(8,128)(2,1)} custom-call(s32[1]{0:T(128)} %bitcast.group_ref, s16[16,128,896]{2,1,0:T(8,128)(2,1)} %bitcast.30, bf16[16,128,640]{2,1,0:T(8,128)(2,1)} %bitcast.32, bf16[768,384]{1,0:T(8,128)(2,1)} %bitcast.34, bf16[384,768]{1,0:T(8,128)(2,1)} %bitcast.36), custom_call_target="tpu_custom_call" | custom-call | tf_op jit(solution)/shard_map/expert/pallas_call | solution.py:216
  120.1 0.0 reduce-scatter.2.cloned.1.call-update
  120.1 0.0 copy-start
  120.1 0.0 copy-start.2
  120.1 0.0 copy-start.3
  120.1 0.0 copy-start.4
  120.1 0.0 copy-start.5
  120.2 8.1 %weight_grads.1 = (bf16[768,384]{1,0:T(8,128)(2,1)}, bf16[384,768]{1,0:T(8,128)(2,1)}) custom-call(s32[1]{0:T(128)} %bitcast.group_ref, s16[16,128,896]{2,1,0:T(8,128)(2,1)} %bitcast.31, bf16[16,128,640]{2,1,0:T(8,128)(2,1)} %bitcast.33, bf16[768,384]{1,0:T(8,128)(2,1)} %bitcast.35, bf16[384,768]{1,0:T(8,128)(2,1)} %bitcast.37), custom_call_target="tpu_custom_call" | custom-call | tf_op jit(solution)/shard_map/weight_grads/pallas_call | solution.py:216
  128.2 68.6 %reduce-scatter.2.cloned.1.call-done = bf16[1,256,768]{2,1,0:T(8,128)(2,1)} async-done(((bf16[16,256,768]{2,1,0:T(8,128)(2,1)}), bf16[1,256,768]{2,1,0:T(8,128)(2,1)}) %reduce-scatter.2.cloned.1.call-update) | async-done | bytes 393232 | tf_op jit(solution)/shard_map/reduce_scatter | solution.py:233
  196.8 0.0 copy-start.1
  196.8 1.0 copy-done.1
  197.8 0.3 restore.1
  198.0 24.0 %all_to_all.11 = bf16[32,8,768]{2,1,0:T(8,128)(2,1)S(1)} all-to-all(bf16[32,8,768]{2,1,0:T(8,128)(2,1)S(1)} %bitcast.20), channel_id=1, replica_groups=mesh['inter'=16,'intra'=32] {'intra'}, dimensions={0} | all-to-all | bytes 786432 | tf_op jit(solution)/shard_map/all_to_all | solution.py:249
  222.1 0.0 copy-done
  222.1 0.0 copy-done.2
  222.1 0.0 copy-done.3
  222.1 0.0 copy-done.4
  222.1 0.0 copy-done.5
  222.1 1.1 pick.1
Async XLA Ops:
  7.2 105.3 %all-gather.5.cloned.1.call-start = ((), (), s32[]{:S(2)}) async-start(), calls=%async_computation.4 | async-start | bytes 2785280 | tf_op jit(solution)/shard_map/all_gather | solution.py:205
  31.1 165.7 %reduce-scatter.2.cloned.1.call-start = ((), (), s32[]{:S(2)}) async-start(), calls=%async_computation.3 | async-start | bytes 6684672 | tf_op jit(solution)/shard_map/reduce_scatter | solution.py:233
  120.1 102.0 %copy-start = (bf16[128,768]{1,0:T(8,128)(2,1)S(1)}, bf16[128,768]{1,0:T(8,128)(2,1)}, u32[]{:S(2)}) copy-start(bf16[128,768]{1,0:T(8,128)(2,1)} %out_grad.3) | copy-start | bytes 589828
  120.1 102.0 %copy-start.2 = (s32[128]{0:T(128)S(1)}, s32[128]{0:T(128)}, u32[]{:S(2)}) copy-start(s32[128]{0:T(128)} %param.9) | copy-start | bytes 1540
  120.1 102.0 %copy-start.3 = (s32[128]{0:T(128)S(1)}, s32[128]{0:T(128)}, u32[]{:S(2)}) copy-start(s32[128]{0:T(128)} %param.10) | copy-start | bytes 1540
  120.1 102.0 %copy-start.4 = (s32[128]{0:T(128)S(1)}, s32[128]{0:T(128)}, u32[]{:S(2)}) copy-start(s32[128]{0:T(128)} %param.11) | copy-start | bytes 1540
  120.1 102.0 %copy-start.5 = (f32[128]{0:T(128)S(1)}, f32[128]{0:T(128)}, u32[]{:S(2)}) copy-start(f32[128]{0:T(128)} %param.12) | copy-start | bytes 1540
  196.8 1.0 copy-start.1
Sparse Core Ops, SparseCore 0:
  31.2 72.4 all-gather.4
  120.2 76.5 reduce-scatter.1

commit v10 on v9

--- a/solution.py
+++ b/solution.py
@@ -14,6 +14,7 @@
 TILE = EGRP * KINDS * CAP
 VMEM_BYTES = 60 * 1024 * 1024
 VMEM_SMALL = 8 * 1024 * 1024
+VMEM_MOST = 52 * 1024 * 1024
 TAIL = 128
 STEPS = 229.0
 OCTAVES = 140.0
@@ -212,7 +213,7 @@
     in_block = pl.BlockSpec((width, hidden_units), whole)
     out_block = pl.BlockSpec((hidden_units, width), whole)
 
-    def over_planes(kernel, name, out_specs, out_shape, scratch):
+    def over_planes(kernel, name, out_specs, out_shape, scratch, grant=VMEM_BYTES):
         return pl.pallas_call(
             kernel,
             grid_spec=pltpu.PrefetchScalarGridSpec(
@@ -223,12 +224,12 @@
                 scratch_shapes=scratch,
             ),
             out_shape=out_shape,
-            compiler_params=params,
+            compiler_params=pltpu.CompilerParams(vmem_limit_bytes=grant),
             name=name,
         )(group, spread_x, spread_g, weight_in, weight_out)
 
     send = over_planes(
-        expert_kernel, "expert", by_plane, jax.ShapeDtypeStruct((inter_size, wide, width), jnp.bfloat16), []
+        expert_kernel, "expert", by_plane, jax.ShapeDtypeStruct((inter_size, wide, width), jnp.bfloat16), [], VMEM_MOST
     )
     summed = lax.psum_scatter(send, "inter", scatter_dimension=0, tiled=True)
     in_weight_grad, out_weight_grad = over_planes(

time: 231 us -> 230 us (level)
  no operation moved by 1% of the time
where the time goes in v10:
time: 230 us
  blocking collectives  125 us (54%)
  waiting for transfers between devices  68.9 us (30%)
  Pallas kernels  20.3 us (9%)
  between operations  14.1 us (6%)
    all_gather x1, blocking collectives, on_device(): spread_x = lax.all_gather(ordered_x[None], 'inter', axis=0, tiled=True)  81 us
    reduce_scatter x1, waiting for transfers between devices, on_device(): summed = lax.psum_scatter(send, 'inter', scatter_dimension=0, tiled=True)  68.8 us
    all_to_all x1, blocking collectives, on_device(): lax.all_to_all(back.reshape(intra_size, TILE, width), 'intra', 0, 0, tile...  23.8 us
    all_to_all x1, blocking collectives, on_device(): lax.all_to_all(placed.reshape(intra_size, TILE, width), 'intra', 0, 0, ti...  20.7 us
    pallas_call x2, Pallas kernels, over_planes(): pl.pallas_call(kernel, grid_spec=pltpu.PrefetchScalarGridSpec(num_scalar_...  15.3 us
  transfers between devices with their start and end apart: 2, of which 1 were waited for; matrix products, arithmetic and copies ran while one was open for 0% of the time, Pallas kernels for 4%

profile of v10, /device:TPU:1, one launch (start us, length us, event | category | flops | bytes accessed | tf_op | source)
XLA Modules:
  0.0 229.9 jit_solution(5837824650298869358)
XLA Ops:
  7.2 0.0 copy-start.1
  7.2 0.0 copy-start
  7.2 0.0 all-gather.5.cloned.1.call-start
  7.2 2.4 %place.1 = bf16[256,768]{1,0:T(8,128)(2,1)} custom-call(bf16[128,768]{1,0:T(8,128)(2,1)} %tokens.1, s32[1,128]{1,0:T(1,128)} %bitcast.26, s32[1,128]{1,0:T(1,128)} %bitcast.28, s32[1,128]{1,0:T(1,128)} %bitcast.30, f32[1,128]{1,0:T(1,128)} %bitcast.32, bf16[128,768]{1,0:T(8,128)(2,1)} %out_grad.3), custom_call_target="tpu_custom_call" | custom-call | tf_op jit(solution)/shard_map/place/pallas_call | solution.py:186
  9.6 20.7 %all_to_all.10 = bf16[32,8,768]{2,1,0:T(8,128)(2,1)S(1)} all-to-all(bf16[32,8,768]{2,1,0:T(8,128)(2,1)} %bitcast.38), channel_id=1, replica_groups=mesh['inter'=16,'intra'=32] {'intra'}, dimensions={0} | all-to-all | bytes 786432 | tf_op jit(solution)/shard_map/all_to_all | solution.py:192
  30.3 0.9 order_gradients.1
  31.2 0.0 all-gather.5.cloned.1.call-update
  31.2 0.0 reduce-scatter.2.cloned.1.call-start
  31.2 0.4 order_codes.1
  31.6 81.0 %all-gather.6 = s16[2048,896]{1,0:T(8,128)(2,1)} all-gather(s16[128,896]{1,0:T(8,128)(2,1)S(1)} %order_codes.1), channel_id=2, replica_groups=mesh['inter'=16,'intra'=32] {'inter'}, dimensions={0}, use_global_device_ids=true | all-gather | bytes 3899392 | tf_op jit(solution)/shard_map/all_gather | solution.py:207
  112.6 0.0 all-gather.5.cloned.1.call-done
  112.6 0.0 copy-done.1
  112.6 0.0 copy-done
  112.6 7.2 %expert.1 = bf16[16,256,768]{2,1,0:T(8,128)(2,1)} custom-call(s32[1]{0:T(128)} %bitcast.group_ref, s16[16,128,896]{2,1,0:T(8,128)(2,1)} %bitcast.34, bf16[16,128,640]{2,1,0:T(8,128)(2,1)} %bitcast.36, bf16[768,384]{1,0:T(8,128)(2,1)S(1)} %bitcast.20, bf16[384,768]{1,0:T(8,128)(2,1)S(1)} %bitcast.22), custom_call_target="tpu_custom_call" | custom-call | tf_op jit(solution)/shard_map/expert/pallas_call | solution.py:217
  119.9 0.0 reduce-scatter.2.cloned.1.call-update
  119.9 0.0 copy-start.2
  119.9 0.0 copy-start.4
  119.9 0.0 copy-start.5
  119.9 0.0 copy-start.6
  119.9 0.0 copy-start.7
  120.0 8.1 %weight_grads.1 = (bf16[768,384]{1,0:T(8,128)(2,1)}, bf16[384,768]{1,0:T(8,128)(2,1)}) custom-call(s32[1]{0:T(128)} %bitcast.group_ref, s16[16,128,896]{2,1,0:T(8,128)(2,1)} %bitcast.35, bf16[16,128,640]{2,1,0:T(8,128)(2,1)} %bitcast.37, bf16[768,384]{1,0:T(8,128)(2,1)} %bitcast.19, bf16[384,768]{1,0:T(8,128)(2,1)} %bitcast.21), custom_call_target="tpu_custom_call" | custom-call | tf_op jit(solution)/shard_map/weight_grads/pallas_call | solution.py:217
  128.0 68.8 %reduce-scatter.2.cloned.1.call-done = bf16[1,256,768]{2,1,0:T(8,128)(2,1)} async-done(((bf16[16,256,768]{2,1,0:T(8,128)(2,1)}), bf16[1,256,768]{2,1,0:T(8,128)(2,1)}) %reduce-scatter.2.cloned.1.call-update) | async-done | bytes 393232 | tf_op jit(solution)/shard_map/reduce_scatter | solution.py:234
  196.8 0.0 copy-start.3
  196.8 1.0 copy-done.3
  197.8 0.3 restore.1
  198.1 23.8 %all_to_all.11 = bf16[32,8,768]{2,1,0:T(8,128)(2,1)S(1)} all-to-all(bf16[32,8,768]{2,1,0:T(8,128)(2,1)S(1)} %bitcast.24), channel_id=1, replica_groups=mesh['inter'=16,'intra'=32] {'intra'}, dimensions={0} | all-to-all | bytes 786432 | tf_op jit(solution)/shard_map/all_to_all | solution.py:250
  221.9 0.0 copy-done.2
  221.9 0.0 copy-done.4
  221.9 0.0 copy-done.5
  221.9 0.0 copy-done.6
  221.9 0.0 copy-done.7
  221.9 1.1 pick.1
Async XLA Ops:
  7.2 105.5 %copy-start.1 = (bf16[1,1,384,768]{3,2,1,0:T(8,128)(2,1)S(1)}, bf16[1,1,384,768]{3,2,1,0:T(8,128)(2,1)}, u32[]{:S(2)}) copy-start(bf16[1,1,384,768]{3,2,1,0:T(8,128)(2,1)} %param.15) | copy-start | bytes 1769476
  7.2 105.4 %copy-start = (bf16[1,1,768,384]{3,2,1,0:T(8,128)(2,1)S(1)}, bf16[1,1,768,384]{3,2,1,0:T(8,128)(2,1)}, u32[]{:S(2)}) copy-start(bf16[1,1,768,384]{3,2,1,0:T(8,128)(2,1)} %param.14) | copy-start | bytes 1769476
  7.2 105.4 %all-gather.5.cloned.1.call-start = ((), (), s32[]{:S(2)}) async-start(), calls=%async_computation.4 | async-start | bytes 2785280 | tf_op jit(solution)/shard_map/all_gather | solution.py:206
  31.2 165.6 %reduce-scatter.2.cloned.1.call-start = ((), (), s32[]{:S(2)}) async-start(), calls=%async_computation.3 | async-start | bytes 6684672 | tf_op jit(solution)/shard_map/reduce_scatter | solution.py:234
  119.9 102.0 %copy-start.2 = (bf16[128,768]{1,0:T(8,128)(2,1)S(1)}, bf16[128,768]{1,0:T(8,128)(2,1)}, u32[]{:S(2)}) copy-start(bf16[128,768]{1,0:T(8,128)(2,1)} %out_grad.3) | copy-start | bytes 589828
  119.9 102.0 %copy-start.4 = (s32[128]{0:T(128)S(1)}, s32[128]{0:T(128)}, u32[]{:S(2)}) copy-start(s32[128]{0:T(128)} %param.9) | copy-start | bytes 1540
  119.9 102.0 %copy-start.5 = (s32[128]{0:T(128)S(1)}, s32[128]{0:T(128)}, u32[]{:S(2)}) copy-start(s32[128]{0:T(128)} %param.10) | copy-start | bytes 1540
  119.9 102.0 %copy-start.6 = (s32[128]{0:T(128)S(1)}, s32[128]{0:T(128)}, u32[]{:S(2)}) copy-start(s32[128]{0:T(128)} %param.11) | copy-start | bytes 1540
  119.9 102.0 %copy-start.7 = (f32[128]{0:T(128)S(1)}, f32[128]{0:T(128)}, u32[]{:S(2)}) copy-start(f32[128]{0:T(128)} %param.12) | copy-start | bytes 1540
  196.8 1.0 copy-start.3
Sparse Core Ops, SparseCore 0:
  31.3 72.1 all-gather.4
  120.0 76.7 reduce-scatter.1

commit v11 on v10

--- a/solution.py
+++ b/solution.py
@@ -183,8 +183,14 @@
     small = pltpu.CompilerParams(vmem_limit_bytes=VMEM_SMALL)
     routing = (expert_ids[None], slot_ids[None], keep_mask[None], gate_prob[None])
 
+    columns = width // 2
+    some = lambda rows: pl.BlockSpec((rows, columns), lambda i: (0, i))
+    one_row = pl.BlockSpec((1, tok_rows), lambda i: (0, 0))
     placed = pl.pallas_call(
         functools.partial(place_kernel, intra_size),
+        grid=(width // columns,),
+        in_specs=[some(tok_rows)] + [one_row] * 4 + [some(tok_rows)],
+        out_specs=some(wide),
         out_shape=jax.ShapeDtypeStruct((wide, width), jnp.bfloat16),
         compiler_params=params,
         name="place",

time: 230 us -> 230 us (level)
  no operation moved by 1% of the time
where the time goes in v11:
time: 230 us
  blocking collectives  124 us (54%)
  waiting for transfers between devices  70.2 us (31%)
  Pallas kernels  20.4 us (9%)
  between operations  14.1 us (6%)
    all_gather x1, blocking collectives, on_device(): spread_x = lax.all_gather(ordered_x[None], 'inter', axis=0, tiled=True)  79.1 us
    reduce_scatter x1, waiting for transfers between devices, on_device(): summed = lax.psum_scatter(send, 'inter', scatter_dimension=0, tiled=True)  70.2 us
    all_to_all x1, blocking collectives, on_device(): lax.all_to_all(back.reshape(intra_size, TILE, width), 'intra', 0, 0, tile...  24.1 us
    all_to_all x1, blocking collectives, on_device(): lax.all_to_all(placed.reshape(intra_size, TILE, width), 'intra', 0, 0, ti...  20.7 us
    pallas_call x2, Pallas kernels, over_planes(): pl.pallas_call(kernel, grid_spec=pltpu.PrefetchScalarGridSpec(num_scalar_...  15.3 us
  transfers between devices with their start and end apart: 2, of which 1 were waited for; matrix products, arithmetic and copies ran while one was open for 0% of the time, Pallas kernels for 4%

profile of v11, /device:TPU:1, one launch (start us, length us, event | category | flops | bytes accessed | tf_op | source)
XLA Modules:
  0.0 229.8 jit_solution(1631250916553017589)
XLA Ops:
  7.2 0.0 copy-start.1
  7.2 0.0 copy-start
  7.2 0.0 all-gather.5.cloned.1.call-start
  7.2 2.4 %place.1 = bf16[256,768]{1,0:T(8,128)(2,1)} custom-call(bf16[128,768]{1,0:T(8,128)(2,1)} %tokens.1, s32[1,128]{1,0:T(1,128)} %bitcast.26, s32[1,128]{1,0:T(1,128)} %bitcast.28, s32[1,128]{1,0:T(1,128)} %bitcast.30, f32[1,128]{1,0:T(1,128)} %bitcast.32, bf16[128,768]{1,0:T(8,128)(2,1)} %out_grad.3), custom_call_target="tpu_custom_call" | custom-call | tf_op jit(solution)/shard_map/place/pallas_call | solution.py:189
  9.7 20.7 %all_to_all.10 = bf16[32,8,768]{2,1,0:T(8,128)(2,1)S(1)} all-to-all(bf16[32,8,768]{2,1,0:T(8,128)(2,1)} %bitcast.38), channel_id=1, replica_groups=mesh['inter'=16,'intra'=32] {'intra'}, dimensions={0} | all-to-all | bytes 786432 | tf_op jit(solution)/shard_map/all_to_all | solution.py:198
  30.3 0.9 order_gradients.1
  31.2 0.0 all-gather.5.cloned.1.call-update
  31.3 0.0 reduce-scatter.2.cloned.1.call-start
  31.3 0.4 order_codes.1
  31.7 79.1 %all-gather.6 = s16[2048,896]{1,0:T(8,128)(2,1)} all-gather(s16[128,896]{1,0:T(8,128)(2,1)S(1)} %order_codes.1), channel_id=2, replica_groups=mesh['inter'=16,'intra'=32] {'inter'}, dimensions={0}, use_global_device_ids=true | all-gather | bytes 3899392 | tf_op jit(solution)/shard_map/all_gather | solution.py:213
  110.8 0.0 all-gather.5.cloned.1.call-done
  110.8 0.0 copy-done.1
  110.8 0.0 copy-done
  110.8 7.2 %expert.1 = bf16[16,256,768]{2,1,0:T(8,128)(2,1)} custom-call(s32[1]{0:T(128)} %bitcast.group_ref, s16[16,128,896]{2,1,0:T(8,128)(2,1)} %bitcast.34, bf16[16,128,640]{2,1,0:T(8,128)(2,1)} %bitcast.36, bf16[768,384]{1,0:T(8,128)(2,1)S(1)} %bitcast.20, bf16[384,768]{1,0:T(8,128)(2,1)S(1)} %bitcast.22), custom_call_target="tpu_custom_call" | custom-call | tf_op jit(solution)/shard_map/expert/pallas_call | solution.py:223
  118.0 0.0 reduce-scatter.2.cloned.1.call-update
  118.1 0.0 copy-start.2
  118.1 0.0 copy-start.4
  118.1 0.0 copy-start.5
  118.1 0.0 copy-start.6
  118.1 0.0 copy-start.7
  118.1 8.1 %weight_grads.1 = (bf16[768,384]{1,0:T(8,128)(2,1)}, bf16[384,768]{1,0:T(8,128)(2,1)}) custom-call(s32[1]{0:T(128)} %bitcast.group_ref, s16[16,128,896]{2,1,0:T(8,128)(2,1)} %bitcast.35, bf16[16,128,640]{2,1,0:T(8,128)(2,1)} %bitcast.37, bf16[768,384]{1,0:T(8,128)(2,1)} %bitcast.19, bf16[384,768]{1,0:T(8,128)(2,1)} %bitcast.21), custom_call_target="tpu_custom_call" | custom-call | tf_op jit(solution)/shard_map/weight_grads/pallas_call | solution.py:223
  126.2 70.2 %reduce-scatter.2.cloned.1.call-done = bf16[1,256,768]{2,1,0:T(8,128)(2,1)} async-done(((bf16[16,256,768]{2,1,0:T(8,128)(2,1)}), bf16[1,256,768]{2,1,0:T(8,128)(2,1)}) %reduce-scatter.2.cloned.1.call-update) | async-done | bytes 393232 | tf_op jit(solution)/shard_map/reduce_scatter | solution.py:240
  196.4 0.0 copy-start.3
  196.4 1.0 copy-done.3
  197.4 0.3 restore.1
  197.6 24.1 %all_to_all.11 = bf16[32,8,768]{2,1,0:T(8,128)(2,1)S(1)} all-to-all(bf16[32,8,768]{2,1,0:T(8,128)(2,1)S(1)} %bitcast.24), channel_id=1, replica_groups=mesh['inter'=16,'intra'=32] {'intra'}, dimensions={0} | all-to-all | bytes 786432 | tf_op jit(solution)/shard_map/all_to_all | solution.py:256
  221.8 0.0 copy-done.2
  221.8 0.0 copy-done.4
  221.8 0.0 copy-done.5
  221.8 0.0 copy-done.6
  221.8 0.0 copy-done.7
  221.8 1.1 pick.1
Async XLA Ops:
  7.2 103.6 %copy-start.1 = (bf16[1,1,384,768]{3,2,1,0:T(8,128)(2,1)S(1)}, bf16[1,1,384,768]{3,2,1,0:T(8,128)(2,1)}, u32[]{:S(2)}) copy-start(bf16[1,1,384,768]{3,2,1,0:T(8,128)(2,1)} %param.15) | copy-start | bytes 1769476
  7.2 103.6 %copy-start = (bf16[1,1,768,384]{3,2,1,0:T(8,128)(2,1)S(1)}, bf16[1,1,768,384]{3,2,1,0:T(8,128)(2,1)}, u32[]{:S(2)}) copy-start(bf16[1,1,768,384]{3,2,1,0:T(8,128)(2,1)} %param.14) | copy-start | bytes 1769476
  7.2 103.6 %all-gather.5.cloned.1.call-start = ((), (), s32[]{:S(2)}) async-start(), calls=%async_computation.4 | async-start | bytes 2785280 | tf_op jit(solution)/shard_map/all_gather | solution.py:212
  31.3 165.1 %reduce-scatter.2.cloned.1.call-start = ((), (), s32[]{:S(2)}) async-start(), calls=%async_computation.3 | async-start | bytes 6684672 | tf_op jit(solution)/shard_map/reduce_scatter | solution.py:240
  118.1 103.7 %copy-start.2 = (bf16[128,768]{1,0:T(8,128)(2,1)S(1)}, bf16[128,768]{1,0:T(8,128)(2,1)}, u32[]{:S(2)}) copy-start(bf16[128,768]{1,0:T(8,128)(2,1)} %out_grad.3) | copy-start | bytes 589828
  118.1 103.7 %copy-start.4 = (s32[128]{0:T(128)S(1)}, s32[128]{0:T(128)}, u32[]{:S(2)}) copy-start(s32[128]{0:T(128)} %param.9) | copy-start | bytes 1540
  118.1 103.7 %copy-start.5 = (s32[128]{0:T(128)S(1)}, s32[128]{0:T(128)}, u32[]{:S(2)}) copy-start(s32[128]{0:T(128)} %param.10) | copy-start | bytes 1540
  118.1 103.7 %copy-start.6 = (s32[128]{0:T(128)S(1)}, s32[128]{0:T(128)}, u32[]{:S(2)}) copy-start(s32[128]{0:T(128)} %param.11) | copy-start | bytes 1540
  118.1 103.7 %copy-start.7 = (f32[128]{0:T(128)S(1)}, f32[128]{0:T(128)}, u32[]{:S(2)}) copy-start(f32[128]{0:T(128)} %param.12) | copy-start | bytes 1540
  196.4 1.0 copy-start.3
Sparse Core Ops, SparseCore 0:
  31.4 71.8 all-gather.4
  118.2 78.1 reduce-scatter.1
